TPU v7x, 512 devices: a whole 4x4x16 slice. The times are simulated.
512 devices in a mesh: row: 4 (over x), col: 4 (over y), dep: 32 (over z, core).
Axes of the slice: x: 4, y: 4, z: 16, core: 2. Of those that a mesh axis runs over, the one named last changes fastest.
Arguments:
- labels: int32 [32, 64, 4096], P('row', 'col', 'dep'), may hold values from 0 to 7, as said below
- conductivity: float32 [8], replicated, may hold values from 0.001 to 20, as said below
Outputs:
- pressure: float32 [3, 32, 64, 4096], P(None, 'row', 'col', 'dep')
- permeability: float32 [3, 3], replicated
Inputs may be any that keep to these rules, and one draw needn't show every extreme that they name: `labels`: each label is a phase index; phases are more frequent toward higher indices along each of the three dimensions. `conductivity`: conductivities are positive.
All inputs are finite; a program needn't handle non-finite values.
Results may differ from a plain program's by a relative error of at most 0.0003.
Values sent between devices are 32-bit elements; how exact they have to be, the bound alone decides.
No kernel may reach another device: no remote copies, remote signals or barrier semaphores. Data moves between devices by JAX's collectives and lax.ppermute only.
A program may use at most 64 MiB of HBM per device.

v0:
```python
import jax
import jax.numpy as jnp
from jax import lax
from jax.sharding import PartitionSpec as P

LEVELS = 4
COARSE = 6


RELAX_WEIGHT = 0.8


def padded_2(x, sides, width):
    for axis, dim in sides:
        peers, length = (lax.axis_size(axis), x.shape[dim])
        up = [(i, (i + 1) % peers) for i in range(peers - 1)]
        down = [(j, i) for i, j in up]
        last = lax.slice_in_dim(x, length - width, length, axis=dim)
        first = lax.slice_in_dim(x, 0, width, axis=dim)
        before = lax.ppermute(last, axis, up)
        after = lax.ppermute(first, axis, down)
        x = jnp.concatenate([before, x, after], axis=dim)
    return x


def cropped(field, margin):
    return field[..., margin:-margin, margin:-margin, margin:-margin]


def shifted(field, axis_no, stride):
    ndims = field.ndim
    result = field
    for spatial in range(3):
        position = ndims - 3 + spatial
        extent = field.shape[position]
        begin = 1 + stride if spatial == axis_no else 1
        result = lax.slice_in_dim(result, begin, begin + extent - 2, axis=position)
    return result


def weights_of(padded_k, level_scale):
    centre = cropped(padded_k, 1)
    weights = []
    for axis_no in range(3):
        for stride in (1, -1):
            beside = shifted(padded_k, axis_no, stride)
            harmonic = 2.0 * centre * beside / (centre + beside)
            weights.append(jnp.where(beside > 0.0, harmonic, centre) * level_scale)
    centre_sum = weights[0]
    for weight in weights[1:]:
        centre_sum = centre_sum + weight
    return (weights, centre_sum)


def apply_op(padded, weights, centre_sum):
    summed = centre_sum * cropped(padded, 1)
    index = 0
    for axis_no in range(3):
        for stride in (1, -1):
            summed = summed - weights[index] * shifted(padded, axis_no, stride)
            index = index + 1
    return summed


def jacobi_sweep(padded, sources, weights, centre_sum):
    return (
        cropped(padded, 1)
        + RELAX_WEIGHT * (sources - apply_op(padded, weights, centre_sum)) / centre_sum
    )


def coarsen(field):
    leading = field.shape[:-3]
    size_x, size_y, size_z = field.shape[-3:]
    reshaped = field.reshape(leading + (size_x // 2, 2, size_y // 2, 2, size_z // 2, 2))
    count = len(leading)
    return jnp.mean(reshaped, axis=(count + 1, count + 3, count + 5))


def refine(field):
    for position in (-3, -2, -1):
        field = jnp.repeat(field, 2, axis=position)
    return field


def spread_halo(fields):
    return padded_2(fields, (("row", 1), ("col", 2), ("dep", 3)), 1)


def weights_at(cell_conduct, level_no):
    padded_k = padded_2(cell_conduct, (("row", 0), ("col", 1), ("dep", 2)), 1)
    return weights_of(padded_k, 0.25**level_no)


def correction(remainder, cell_conduct, level_no):
    coarse_k = coarsen(cell_conduct)
    coarse_sources = coarsen(remainder)
    weights, centre_sum = weights_at(coarse_k, level_no + 1)
    coarse_fix = vcycle(coarse_sources, coarse_k, weights, centre_sum, level_no + 1)
    return refine(coarse_fix)


def vcycle(sources, cell_conduct, weights, centre_sum, level_no):
    iterate = RELAX_WEIGHT * sources / centre_sum
    if level_no == LEVELS - 1:
        for counter in range(COARSE - 1):
            iterate = jacobi_sweep(spread_halo(iterate), sources, weights, centre_sum)
        return iterate
    iterate = jacobi_sweep(spread_halo(iterate), sources, weights, centre_sum)
    remainder = sources - apply_op(spread_halo(iterate), weights, centre_sum)
    iterate = iterate + correction(remainder, cell_conduct, level_no)
    for counter in range(2):
        iterate = jacobi_sweep(spread_halo(iterate), sources, weights, centre_sum)
    return iterate


def body(labels, conductivity):
    cell_conduct = jnp.zeros(labels.shape, jnp.float32)
    for phase in range(conductivity.shape[0]):
        cell_conduct = cell_conduct + jnp.where(labels == phase, conductivity[phase], 0.0)
    inner_weights, inner_sum = weights_at(cell_conduct, 0)
    sources = jnp.stack(
        [inner_weights[2 * solve_no + 1] - inner_weights[2 * solve_no] for solve_no in range(3)]
    )
    pressure = vcycle(sources, cell_conduct, inner_weights, inner_sum, 0)
    padded = spread_halo(pressure)
    centre = cropped(padded, 1)
    tensor_rows = []
    for axis_no in range(3):
        unit_vec = (jnp.arange(3) == axis_no).astype(jnp.float32)[:, None, None, None]
        rising = shifted(padded, axis_no, 1) - centre + unit_vec
        falling = centre - shifted(padded, axis_no, -1) + unit_vec
        fluxes = 0.5 * (
            inner_weights[2 * axis_no] * rising + inner_weights[2 * axis_no + 1] * falling
        )
        tensor_rows.append(jnp.sum(fluxes, axis=(1, 2, 3)))
    partial_sums = jnp.stack(tensor_rows)
    summed = lax.psum(partial_sums, ("row", "col", "dep"))
    cell_count = (
        pressure.shape[1]
        * pressure.shape[2]
        * pressure.shape[3]
        * lax.axis_size("row")
        * lax.axis_size("col")
        * lax.axis_size("dep")
    )
    return (pressure, summed / cell_count)


def solution(mesh):
    in_specs = (P("row", "col", "dep"), P())
    out_specs = (P(None, "row", "col", "dep"), P())
    return jax.shard_map(body, mesh=mesh, in_specs=in_specs, out_specs=out_specs, check_vma=False)
```

profile of v0, /device:TPU:1, one launch (start us, length us, event | category | flops | bytes accessed | tf_op | source)
XLA Modules:
  0.0 669.6 jit_solution(18301596187018859586)
XLA Ops:
  2.2 5.8 select_add_fusion
  8.0 3.9 collective-permute-start
  13.3 5.6 reshape.157
  22.7 4.0 collective-permute-start.2
  27.6 7.3 %collective-permute-start.5 = (f32[10,18,1]{2,1,0:T(8,128)S(1)}, f32[10,18,1]{2,1,0:T(8,128)S(1)}, u32[]{:S(2)}, u32[]{:S(2)}) collective-permute-start(f32[10,18,1]{2,1,0:T(8,128)S(1)} %get-tuple-element.89), channel_id=1, source_target_pairs={{1,0},{2,1},{3,2},{4,3},{5,4},{6,5},{7,6},{8,7},{9,8},{10,9},{11,1... | collective-permute-start | bytes 2168 | tf_op jit(solution)/shard_map/ppermute | solution.py:21
  40.2 4.9 collective-permute-start.7
  51.8 4.5 collective-permute-start.9
  57.4 6.0 collective-permute-start.11
  66.7 4.5 collective-permute-start.21
  73.9 4.9 collective-permute-start.13
  81.1 4.5 collective-permute-start.15
  98.6 4.4 collective-permute-done.16
  103.3 13.9 %reshape.156 = f32[3,4,2,8,2,64,2]{6,5,4,3,2,1,0:T(8,128)} reshape(f32[3,8,16,128]{3,2,1,0:T(8,128)S(1)} %fusion.61) | data formatting | bytes 393216 | tf_op jit(solution)/shard_map/reshape | solution.py:75
  117.2 5.5 reduce_sum.95
  124.0 4.6 collective-permute-start.25
  137.3 4.0 collective-permute-start.37
  149.3 4.0 collective-permute-start.29
  154.7 4.3 collective-permute-start.39
  160.5 4.9 collective-permute-start.31
  171.6 4.1 collective-permute-start.41
  191.0 4.5 collective-permute-start.43
  197.7 4.0 collective-permute-start.45
  202.5 6.3 collective-permute-start.47
  212.1 4.5 collective-permute-start.57
  218.1 4.5 collective-permute-start.49
  224.7 4.0 collective-permute-start.51
  230.7 5.5 collective-permute-start.59
  240.8 4.3 collective-permute-done.52
  246.8 4.6 collective-permute-start.61
  253.4 4.3 collective-permute-start.63
  268.6 4.5 collective-permute-start.67
  275.2 4.5 collective-permute-start.69
  280.6 5.5 collective-permute-start.71
  288.0 4.2 collective-permute-done.70
  293.6 4.2 collective-permute-start.73
  299.9 4.2 collective-permute-start.75
  305.0 6.6 collective-permute-start.77
  318.1 4.5 collective-permute-start.79
  324.7 4.5 collective-permute-start.81
  330.1 4.6 collective-permute-start.83
  341.1 4.5 collective-permute-start.85
  347.7 4.5 collective-permute-start.87
  353.1 4.8 collective-permute-start.89
  364.6 4.5 collective-permute-start.91
  371.2 4.5 collective-permute-start.93
  376.6 4.8 collective-permute-start.95
  388.3 4.5 collective-permute-start.97
  395.0 4.5 collective-permute-start.99
  400.4 4.6 collective-permute-start.101
  412.2 4.5 collective-permute-start.103
  428.3 4.9 collective-permute-start.107
  436.5 4.5 collective-permute-start.109
  452.3 6.3 collective-permute-start.113
  464.4 4.5 collective-permute-start.115
  471.2 4.3 collective-permute-start.117
  476.5 6.0 collective-permute-start.119
  487.0 4.4 collective-permute-done.118
  493.1 4.9 collective-permute-start.121
  500.2 4.5 collective-permute-start.123
  513.4 5.1 collective-permute-done.124
  520.2 4.3 collective-permute-start.127
  526.7 4.4 collective-permute-start.129
  539.8 5.0 collective-permute-done.130
  545.2 123.9 %psum.7 = f32[3,3]{1,0:T(4,128)S(1)} all-reduce(f32[3,3]{1,0:T(4,128)S(1)} %pad_maximum_fusion.401), channel_id=1, replica_groups=mesh['row'=4,'col'=4,'dep'=32] {'row','col','dep'}, use_global_device_ids=true, to_apply=%region_11.12 | all-reduce | flops 9 | bytes 72 | tf_op jit(solution)/shard_map/psum | solution.py:138
  (379 shorter events, 233.9 us)
Async XLA Ops:
  8.0 13.4 %collective-permute-start = (f32[1,16,128]{2,1,0:T(8,128)S(1)}, f32[1,16,128]{2,1,0:T(8,128)S(1)}, u32[]{:S(2)}, u32[]{:S(2)}) collective-permute-start(f32[1,16,128]{2,1,0:T(8,128)S(1)} %get-tuple-element.103), channel_id=1, source_target_pairs={{0,128},{128,256},{256,384},{1,129},{129,257},{257,385},{2,130},{1... | collective-permute-start | bytes 24584 | tf_op jit(solution)/shard_map/ppermute | solution.py:20
  12.0 9.5 %collective-permute-start.1 = (f32[1,16,128]{2,1,0:T(8,128)S(1)}, f32[1,16,128]{2,1,0:T(8,128)S(1)}, u32[]{:S(2)}, u32[]{:S(2)}) collective-permute-start(f32[1,16,128]{2,1,0:T(8,128)S(1)} %get-tuple-element.104), channel_id=1, source_target_pairs={{128,0},{256,128},{384,256},{129,1},{257,129},{385,257},{130,2},{2... | collective-permute-start | bytes 24584 | tf_op jit(solution)/shard_map/ppermute | solution.py:21
  27.6 9.3 %collective-permute-start.5 = (f32[10,18,1]{2,1,0:T(8,128)S(1)}, f32[10,18,1]{2,1,0:T(8,128)S(1)}, u32[]{:S(2)}, u32[]{:S(2)}) collective-permute-start(f32[10,18,1]{2,1,0:T(8,128)S(1)} %get-tuple-element.89), channel_id=1, source_target_pairs={{1,0},{2,1},{3,2},{4,3},{5,4},{6,5},{7,6},{8,7},{9,8},{10,9},{11,1... | collective-permute-start | bytes 2168 | tf_op jit(solution)/shard_map/ppermute | solution.py:21
  38.9 11.5 %collective-permute-start.6 = (f32[3,1,16,128]{3,2,1,0:T(8,128)S(1)}, f32[3,1,16,128]{3,2,1,0:T(8,128)S(1)}, u32[]{:S(2)}, u32[]{:S(2)}) collective-permute-start(f32[3,1,16,128]{3,2,1,0:T(8,128)S(1)} %get-tuple-element.71), channel_id=1, source_target_pairs={{128,0},{256,128},{384,256},{129,1},{257,129},{385,257},{130,2},{2... | collective-permute-start | bytes 73736 | tf_op jit(solution)/shard_map/ppermute | solution.py:21
  40.2 10.3 %collective-permute-start.7 = (f32[3,1,16,128]{3,2,1,0:T(8,128)S(1)}, f32[3,1,16,128]{3,2,1,0:T(8,128)S(1)}, u32[]{:S(2)}, u32[]{:S(2)}) collective-permute-start(f32[3,1,16,128]{3,2,1,0:T(8,128)S(1)} %get-tuple-element.70), channel_id=1, source_target_pairs={{0,128},{128,256},{256,384},{1,129},{129,257},{257,385},{2,130},{1... | collective-permute-start | bytes 73736 | tf_op jit(solution)/shard_map/ppermute | solution.py:20
  45.1 20.3 %collective-permute-start.19 = (f32[1,8,64]{2,1,0:T(8,128)S(1)}, f32[1,8,64]{2,1,0:T(8,128)S(1)}, u32[]{:S(2)}, u32[]{:S(2)}) collective-permute-start(f32[1,8,64]{2,1,0:T(8,128)S(1)} %get-tuple-element.146), channel_id=1, source_target_pairs={{0,128},{128,256},{256,384},{1,129},{129,257},{257,385},{2,130},{1... | collective-permute-start | bytes 6152 | tf_op jit(solution)/shard_map/ppermute | solution.py:20
  48.5 16.9 %collective-permute-start.18 = (f32[1,8,64]{2,1,0:T(8,128)S(1)}, f32[1,8,64]{2,1,0:T(8,128)S(1)}, u32[]{:S(2)}, u32[]{:S(2)}) collective-permute-start(f32[1,8,64]{2,1,0:T(8,128)S(1)} %get-tuple-element.145), channel_id=1, source_target_pairs={{128,0},{256,128},{384,256},{129,1},{257,129},{385,257},{130,2},{2... | collective-permute-start | bytes 6152 | tf_op jit(solution)/shard_map/ppermute | solution.py:21
  50.5 6.0 collective-permute-start.8
  57.4 13.9 %collective-permute-start.11 = (f32[3,10,18,1]{3,2,1,0:T(8,128)S(1)}, f32[3,10,18,1]{3,2,1,0:T(8,128)S(1)}, u32[]{:S(2)}, u32[]{:S(2)}) collective-permute-start(f32[3,10,18,1]{3,2,1,0:T(8,128)S(1)} %get-tuple-element.51), channel_id=1, source_target_pairs={{0,1},{1,2},{2,3},{3,4},{4,5},{5,6},{6,7},{7,8},{8,9},{9,10},{10,1... | collective-permute-start | bytes 6488 | tf_op jit(solution)/shard_map/ppermute | solution.py:20
  63.5 8.8 %collective-permute-start.10 = (f32[3,10,18,1]{3,2,1,0:T(8,128)S(1)}, f32[3,10,18,1]{3,2,1,0:T(8,128)S(1)}, u32[]{:S(2)}, u32[]{:S(2)}) collective-permute-start(f32[3,10,18,1]{3,2,1,0:T(8,128)S(1)} %get-tuple-element.50), channel_id=1, source_target_pairs={{1,0},{2,1},{3,2},{4,3},{5,4},{6,5},{7,6},{8,7},{9,8},{10,9},{11,1... | collective-permute-start | bytes 6488 | tf_op jit(solution)/shard_map/ppermute | solution.py:21
  65.4 13.4 %collective-permute-start.20 = (f32[6,1,64]{2,1,0:T(1,128)S(1)}, f32[6,1,64]{2,1,0:T(1,128)S(1)}, u32[]{:S(2)}, u32[]{:S(2)}) collective-permute-start(f32[6,1,64]{2,1,0:T(1,128)S(1)} %get-tuple-element.132), channel_id=1, source_target_pairs={{32,0},{64,32},{96,64},{33,1},{65,33},{97,65},{34,2},{66,34},{98,6... | collective-permute-start | bytes 4616 | tf_op jit(solution)/shard_map/ppermute | solution.py:21
  66.7 12.1 %collective-permute-start.21 = (f32[6,1,64]{2,1,0:T(1,128)S(1)}, f32[6,1,64]{2,1,0:T(1,128)S(1)}, u32[]{:S(2)}, u32[]{:S(2)}) collective-permute-start(f32[6,1,64]{2,1,0:T(1,128)S(1)} %get-tuple-element.131), channel_id=1, source_target_pairs={{0,32},{32,64},{64,96},{1,33},{33,65},{65,97},{2,34},{34,66},{66,9... | collective-permute-start | bytes 4616 | tf_op jit(solution)/shard_map/ppermute | solution.py:20
  72.6 6.3 collective-permute-start.12
  79.8 11.7 %collective-permute-start.14 = (f32[3,10,1,128]{3,2,1,0:T(1,128)S(1)}, f32[3,10,1,128]{3,2,1,0:T(1,128)S(1)}, u32[]{:S(2)}, u32[]{:S(2)}) collective-permute-start(f32[3,10,1,128]{3,2,1,0:T(1,128)S(1)} %get-tuple-element.59), channel_id=1, source_target_pairs={{32,0},{64,32},{96,64},{33,1},{65,33},{97,65},{34,2},{66,34},{98,6... | collective-permute-start | bytes 46088 | tf_op jit(solution)/shard_map/ppermute | solution.py:21
  81.1 10.4 %collective-permute-start.15 = (f32[3,10,1,128]{3,2,1,0:T(1,128)S(1)}, f32[3,10,1,128]{3,2,1,0:T(1,128)S(1)}, u32[]{:S(2)}, u32[]{:S(2)}) collective-permute-start(f32[3,10,1,128]{3,2,1,0:T(1,128)S(1)} %get-tuple-element.58), channel_id=1, source_target_pairs={{0,32},{32,64},{64,96},{1,33},{33,65},{65,97},{2,34},{34,66},{66,9... | collective-permute-start | bytes 46088 | tf_op jit(solution)/shard_map/ppermute | solution.py:20
  85.7 10.4 %collective-permute-start.22 = (f32[6,10,1]{2,1,0:T(8,128)S(1)}, f32[6,10,1]{2,1,0:T(8,128)S(1)}, u32[]{:S(2)}, u32[]{:S(2)}) collective-permute-start(f32[6,10,1]{2,1,0:T(8,128)S(1)} %get-tuple-element.122), channel_id=1, source_target_pairs={{1,0},{2,1},{3,2},{4,3},{5,4},{6,5},{7,6},{8,7},{9,8},{10,9},{11,1... | collective-permute-start | bytes 728 | tf_op jit(solution)/shard_map/ppermute | solution.py:21
  87.6 8.5 %collective-permute-start.23 = (f32[6,10,1]{2,1,0:T(8,128)S(1)}, f32[6,10,1]{2,1,0:T(8,128)S(1)}, u32[]{:S(2)}, u32[]{:S(2)}) collective-permute-start(f32[6,10,1]{2,1,0:T(8,128)S(1)} %get-tuple-element.121), channel_id=1, source_target_pairs={{0,1},{1,2},{2,3},{3,4},{4,5},{5,6},{6,7},{7,8},{8,9},{9,10},{10,1... | collective-permute-start | bytes 728 | tf_op jit(solution)/shard_map/ppermute | solution.py:20
  91.7 6.8 %collective-permute-start.17 = (f32[3,10,18,1]{3,2,1,0:T(8,128)S(1)}, f32[3,10,18,1]{3,2,1,0:T(8,128)S(1)}, u32[]{:S(2)}, u32[]{:S(2)}) collective-permute-start(f32[3,10,18,1]{3,2,1,0:T(8,128)S(1)} %get-tuple-element.49), channel_id=1, source_target_pairs={{0,1},{1,2},{2,3},{3,4},{4,5},{5,6},{6,7},{7,8},{8,9},{9,10},{10,1... | collective-permute-start | bytes 6488 | tf_op jit(solution)/shard_map/ppermute | solution.py:20
  94.2 8.8 %collective-permute-start.16 = (f32[3,10,18,1]{3,2,1,0:T(8,128)S(1)}, f32[3,10,18,1]{3,2,1,0:T(8,128)S(1)}, u32[]{:S(2)}, u32[]{:S(2)}) collective-permute-start(f32[3,10,18,1]{3,2,1,0:T(8,128)S(1)} %get-tuple-element.48), channel_id=1, source_target_pairs={{1,0},{2,1},{3,2},{4,3},{5,4},{6,5},{7,6},{8,7},{9,8},{10,9},{11,1... | collective-permute-start | bytes 6488 | tf_op jit(solution)/shard_map/ppermute | solution.py:21
  122.7 10.8 %collective-permute-start.24 = (f32[3,1,8,64]{3,2,1,0:T(8,128)S(1)}, f32[3,1,8,64]{3,2,1,0:T(8,128)S(1)}, u32[]{:S(2)}, u32[]{:S(2)}) collective-permute-start(f32[3,1,8,64]{3,2,1,0:T(8,128)S(1)} %get-tuple-element.120), channel_id=1, source_target_pairs={{128,0},{256,128},{384,256},{129,1},{257,129},{385,257},{130,2},{2... | collective-permute-start | bytes 18440 | tf_op jit(solution)/shard_map/ppermute | solution.py:21
  124.0 9.5 %collective-permute-start.25 = (f32[3,1,8,64]{3,2,1,0:T(8,128)S(1)}, f32[3,1,8,64]{3,2,1,0:T(8,128)S(1)}, u32[]{:S(2)}, u32[]{:S(2)}) collective-permute-start(f32[3,1,8,64]{3,2,1,0:T(8,128)S(1)} %get-tuple-element.119), channel_id=1, source_target_pairs={{0,128},{128,256},{256,384},{1,129},{129,257},{257,385},{2,130},{1... | collective-permute-start | bytes 18440 | tf_op jit(solution)/shard_map/ppermute | solution.py:20
  128.6 67.0 %collective-permute-start.55 = (f32[1,2,16]{2,1,0:T(2,128)S(1)}, f32[1,2,16]{2,1,0:T(2,128)S(1)}, u32[]{:S(2)}, u32[]{:S(2)}) collective-permute-start(f32[1,2,16]{2,1,0:T(2,128)S(1)} %multiply_bitcast_fusion), channel_id=1, source_target_pairs={{0,128},{128,256},{256,384},{1,129},{129,257},{257,385},{2,130},{1... | collective-permute-start | bytes 392 | tf_op jit(solution)/shard_map/ppermute | solution.py:20
  132.3 63.3 %collective-permute-start.54 = (f32[1,2,16]{2,1,0:T(2,128)S(1)}, f32[1,2,16]{2,1,0:T(2,128)S(1)}, u32[]{:S(2)}, u32[]{:S(2)}) collective-permute-start(f32[1,2,16]{2,1,0:T(2,128)S(1)} %multiply_bitcast_fusion), channel_id=1, source_target_pairs={{128,0},{256,128},{384,256},{129,1},{257,129},{385,257},{130,2},{2... | collective-permute-start | bytes 392 | tf_op jit(solution)/shard_map/ppermute | solution.py:21
  133.6 9.0 %collective-permute-start.27 = (f32[3,6,1,64]{3,2,1,0:T(1,128)S(1)}, f32[3,6,1,64]{3,2,1,0:T(1,128)S(1)}, u32[]{:S(2)}, u32[]{:S(2)}) collective-permute-start(f32[3,6,1,64]{3,2,1,0:T(1,128)S(1)} %get-tuple-element.102), channel_id=1, source_target_pairs={{0,32},{32,64},{64,96},{1,33},{33,65},{65,97},{2,34},{34,66},{66,9... | collective-permute-start | bytes 13832 | tf_op jit(solution)/shard_map/ppermute | solution.py:20
  137.3 12.0 %collective-permute-start.37 = (f32[1,4,32]{2,1,0:T(4,128)S(1)}, f32[1,4,32]{2,1,0:T(4,128)S(1)}, u32[]{:S(2)}, u32[]{:S(2)}) collective-permute-start(f32[1,4,32]{2,1,0:T(4,128)S(1)} %get-tuple-element.172), channel_id=1, source_target_pairs={{0,128},{128,256},{256,384},{1,129},{129,257},{257,385},{2,130},{1... | collective-permute-start | bytes 1544 | tf_op jit(solution)/shard_map/ppermute | solution.py:20
  141.3 12.1 %collective-permute-start.36 = (f32[1,4,32]{2,1,0:T(4,128)S(1)}, f32[1,4,32]{2,1,0:T(4,128)S(1)}, u32[]{:S(2)}, u32[]{:S(2)}) collective-permute-start(f32[1,4,32]{2,1,0:T(4,128)S(1)} %get-tuple-element.171), channel_id=1, source_target_pairs={{128,0},{256,128},{384,256},{129,1},{257,129},{385,257},{130,2},{2... | collective-permute-start | bytes 1544 | tf_op jit(solution)/shard_map/ppermute | solution.py:21
  147.4 7.3 %collective-permute-start.28 = (f32[3,6,10,1]{3,1,2,0:T(8,128)S(1)}, f32[3,6,10,1]{3,1,2,0:T(8,128)S(1)}, u32[]{:S(2)}, u32[]{:S(2)}) collective-permute-start(f32[3,6,10,1]{3,1,2,0:T(8,128)S(1)} %get-tuple-element.86), channel_id=1, source_target_pairs={{1,0},{2,1},{3,2},{4,3},{5,4},{6,5},{7,6},{8,7},{9,8},{10,9},{11,1... | collective-permute-start | bytes 2168 | tf_op jit(solution)/shard_map/ppermute | solution.py:21
  149.3 9.6 %collective-permute-start.29 = (f32[3,6,10,1]{3,1,2,0:T(8,128)S(1)}, f32[3,6,10,1]{3,1,2,0:T(8,128)S(1)}, u32[]{:S(2)}, u32[]{:S(2)}) collective-permute-start(f32[3,6,10,1]{3,1,2,0:T(8,128)S(1)} %get-tuple-element.87), channel_id=1, source_target_pairs={{0,1},{1,2},{2,3},{3,4},{4,5},{5,6},{6,7},{7,8},{8,9},{9,10},{10,1... | collective-permute-start | bytes 2168 | tf_op jit(solution)/shard_map/ppermute | solution.py:20
  153.4 7.1 %collective-permute-start.38 = (f32[4,1,32]{2,1,0:T(1,128)S(1)}, f32[4,1,32]{2,1,0:T(1,128)S(1)}, u32[]{:S(2)}, u32[]{:S(2)}) collective-permute-start(f32[4,1,32]{2,1,0:T(1,128)S(1)} %get-tuple-element.166), channel_id=1, source_target_pairs={{32,0},{64,32},{96,64},{33,1},{65,33},{97,65},{34,2},{66,34},{98,6... | collective-permute-start | bytes 1544 | tf_op jit(solution)/shard_map/ppermute | solution.py:21
  154.7 10.7 %collective-permute-start.39 = (f32[4,1,32]{2,1,0:T(1,128)S(1)}, f32[4,1,32]{2,1,0:T(1,128)S(1)}, u32[]{:S(2)}, u32[]{:S(2)}) collective-permute-start(f32[4,1,32]{2,1,0:T(1,128)S(1)} %get-tuple-element.165), channel_id=1, source_target_pairs={{0,32},{32,64},{64,96},{1,33},{33,65},{65,97},{2,34},{34,66},{66,9... | collective-permute-start | bytes 1544 | tf_op jit(solution)/shard_map/ppermute | solution.py:20
  159.2 6.3 collective-permute-start.30
  166.3 9.5 %collective-permute-start.33 = (f32[3,6,1,64]{3,2,1,0:T(1,128)S(1)}, f32[3,6,1,64]{3,2,1,0:T(1,128)S(1)}, u32[]{:S(2)}, u32[]{:S(2)}) collective-permute-start(f32[3,6,1,64]{3,2,1,0:T(1,128)S(1)} %get-tuple-element.100), channel_id=1, source_target_pairs={{0,32},{32,64},{64,96},{1,33},{33,65},{65,97},{2,34},{34,66},{66,9... | collective-permute-start | bytes 13832 | tf_op jit(solution)/shard_map/ppermute | solution.py:20
  169.7 12.5 %collective-permute-start.40 = (f32[4,6,1]{2,1,0:T(8,128)S(1)}, f32[4,6,1]{2,1,0:T(8,128)S(1)}, u32[]{:S(2)}, u32[]{:S(2)}) collective-permute-start(f32[4,6,1]{2,1,0:T(8,128)S(1)} %get-tuple-element.144), channel_id=1, source_target_pairs={{1,0},{2,1},{3,2},{4,3},{5,4},{6,5},{7,6},{8,7},{9,8},{10,9},{11,1... | collective-permute-start | bytes 296 | tf_op jit(solution)/shard_map/ppermute | solution.py:21
  171.6 14.2 %collective-permute-start.41 = (f32[4,6,1]{2,1,0:T(8,128)S(1)}, f32[4,6,1]{2,1,0:T(8,128)S(1)}, u32[]{:S(2)}, u32[]{:S(2)}) collective-permute-start(f32[4,6,1]{2,1,0:T(8,128)S(1)} %get-tuple-element.143), channel_id=1, source_target_pairs={{0,1},{1,2},{2,3},{3,4},{4,5},{5,6},{6,7},{7,8},{8,9},{9,10},{10,1... | collective-permute-start | bytes 296 | tf_op jit(solution)/shard_map/ppermute | solution.py:20
  180.2 6.2 collective-permute-start.34
  189.7 5.9 collective-permute-start.42
  202.5 14.1 %collective-permute-start.47 = (f32[3,4,6,1]{3,2,1,0:T(8,128)S(1)}, f32[3,4,6,1]{3,2,1,0:T(8,128)S(1)}, u32[]{:S(2)}, u32[]{:S(2)}) collective-permute-start(f32[3,4,6,1]{3,2,1,0:T(8,128)S(1)} %get-tuple-element.116), channel_id=1, source_target_pairs={{0,1},{1,2},{2,3},{3,4},{4,5},{5,6},{6,7},{7,8},{8,9},{9,10},{10,1... | collective-permute-start | bytes 872 | tf_op jit(solution)/shard_map/ppermute | solution.py:20
  208.8 7.8 %collective-permute-start.46 = (f32[3,4,6,1]{3,2,1,0:T(8,128)S(1)}, f32[3,4,6,1]{3,2,1,0:T(8,128)S(1)}, u32[]{:S(2)}, u32[]{:S(2)}) collective-permute-start(f32[3,4,6,1]{3,2,1,0:T(8,128)S(1)} %get-tuple-element.115), channel_id=1, source_target_pairs={{1,0},{2,1},{3,2},{4,3},{5,4},{6,5},{7,6},{8,7},{9,8},{10,9},{11,1... | collective-permute-start | bytes 872 | tf_op jit(solution)/shard_map/ppermute | solution.py:21
  210.8 11.9 %collective-permute-start.56 = (f32[3,1,16]{2,1,0:T(1,128)S(1)}, f32[3,1,16]{2,1,0:T(1,128)S(1)}, u32[]{:S(2)}, u32[]{:S(2)}) collective-permute-start(f32[3,1,16]{2,1,0:T(1,128)S(1)} %get-tuple-element.174), channel_id=1, source_target_pairs={{32,0},{64,32},{96,64},{33,1},{65,33},{97,65},{34,2},{66,34},{98,6... | collective-permute-start | bytes 584 | tf_op jit(solution)/shard_map/ppermute | solution.py:21
  212.1 10.6 %collective-permute-start.57 = (f32[3,1,16]{2,1,0:T(1,128)S(1)}, f32[3,1,16]{2,1,0:T(1,128)S(1)}, u32[]{:S(2)}, u32[]{:S(2)}) collective-permute-start(f32[3,1,16]{2,1,0:T(1,128)S(1)} %get-tuple-element.173), channel_id=1, source_target_pairs={{0,32},{32,64},{64,96},{1,33},{33,65},{65,97},{2,34},{34,66},{66,9... | collective-permute-start | bytes 584 | tf_op jit(solution)/shard_map/ppermute | solution.py:20
  216.8 5.9 collective-permute-start.48
  223.4 12.8 %collective-permute-start.50 = (f32[3,4,1,32]{3,2,1,0:T(1,128)S(1)}, f32[3,4,1,32]{3,2,1,0:T(1,128)S(1)}, u32[]{:S(2)}, u32[]{:S(2)}) collective-permute-start(f32[3,4,1,32]{3,2,1,0:T(1,128)S(1)} %get-tuple-element.128), channel_id=1, source_target_pairs={{32,0},{64,32},{96,64},{33,1},{65,33},{97,65},{34,2},{66,34},{98,6... | collective-permute-start | bytes 4616 | tf_op jit(solution)/shard_map/ppermute | solution.py:21
  224.7 11.5 %collective-permute-start.51 = (f32[3,4,1,32]{3,2,1,0:T(1,128)S(1)}, f32[3,4,1,32]{3,2,1,0:T(1,128)S(1)}, u32[]{:S(2)}, u32[]{:S(2)}) collective-permute-start(f32[3,4,1,32]{3,2,1,0:T(1,128)S(1)} %get-tuple-element.127), channel_id=1, source_target_pairs={{0,32},{32,64},{64,96},{1,33},{33,65},{65,97},{2,34},{34,66},{66,9... | collective-permute-start | bytes 4616 | tf_op jit(solution)/shard_map/ppermute | solution.py:20
  228.8 11.9 %collective-permute-start.58 = (f32[3,4,1]{2,1,0:T(4,128)S(1)}, f32[3,4,1]{2,1,0:T(4,128)S(1)}, u32[]{:S(2)}, u32[]{:S(2)}) collective-permute-start(f32[3,4,1]{2,1,0:T(4,128)S(1)} %get-tuple-element.168), channel_id=1, source_target_pairs={{1,0},{2,1},{3,2},{4,3},{5,4},{6,5},{7,6},{8,7},{9,8},{10,9},{11,1... | collective-permute-start | bytes 152 | tf_op jit(solution)/shard_map/ppermute | solution.py:21
  230.7 10.0 %collective-permute-start.59 = (f32[3,4,1]{2,1,0:T(4,128)S(1)}, f32[3,4,1]{2,1,0:T(4,128)S(1)}, u32[]{:S(2)}, u32[]{:S(2)}) collective-permute-start(f32[3,4,1]{2,1,0:T(4,128)S(1)} %get-tuple-element.167), channel_id=1, source_target_pairs={{0,1},{1,2},{2,3},{3,4},{4,5},{5,6},{6,7},{7,8},{8,9},{9,10},{10,1... | collective-permute-start | bytes 152 | tf_op jit(solution)/shard_map/ppermute | solution.py:20
  238.7 6.4 collective-permute-start.52
  280.6 7.5 %collective-permute-start.71 = (f32[3,3,4,1]{3,2,0,1:T(4,128)S(1)}, f32[3,3,4,1]{3,2,0,1:T(4,128)S(1)}, u32[]{:S(2)}, u32[]{:S(2)}) collective-permute-start(f32[3,3,4,1]{3,2,0,1:T(4,128)S(1)} %get-tuple-element.140), channel_id=1, source_target_pairs={{0,1},{1,2},{2,3},{3,4},{4,5},{5,6},{6,7},{7,8},{8,9},{9,10},{10,1... | collective-permute-start | bytes 440 | tf_op jit(solution)/shard_map/ppermute | solution.py:20
  286.1 6.1 collective-permute-start.70
  305.0 8.6 %collective-permute-start.77 = (f32[3,3,4,1]{3,2,0,1:T(4,128)S(1)}, f32[3,3,4,1]{3,2,0,1:T(4,128)S(1)}, u32[]{:S(2)}, u32[]{:S(2)}) collective-permute-start(f32[3,3,4,1]{3,2,0,1:T(4,128)S(1)} %get-tuple-element.138), channel_id=1, source_target_pairs={{0,1},{1,2},{2,3},{3,4},{4,5},{5,6},{6,7},{7,8},{8,9},{9,10},{10,1... | collective-permute-start | bytes 440 | tf_op jit(solution)/shard_map/ppermute | solution.py:20
  330.1 6.5 collective-permute-start.83
  353.1 6.8 %collective-permute-start.89 = (f32[3,3,4,1]{3,2,0,1:T(4,128)S(1)}, f32[3,3,4,1]{3,2,0,1:T(4,128)S(1)}, u32[]{:S(2)}, u32[]{:S(2)}) collective-permute-start(f32[3,3,4,1]{3,2,0,1:T(4,128)S(1)} %get-tuple-element.134), channel_id=1, source_target_pairs={{0,1},{1,2},{2,3},{3,4},{4,5},{5,6},{6,7},{7,8},{8,9},{9,10},{10,1... | collective-permute-start | bytes 440 | tf_op jit(solution)/shard_map/ppermute | solution.py:20
  376.6 6.8 %collective-permute-start.95 = (f32[3,4,6,1]{3,2,1,0:T(8,128)S(1)}, f32[3,4,6,1]{3,2,1,0:T(8,128)S(1)}, u32[]{:S(2)}, u32[]{:S(2)}) collective-permute-start(f32[3,4,6,1]{3,2,1,0:T(8,128)S(1)} %get-tuple-element.112), channel_id=1, source_target_pairs={{0,1},{1,2},{2,3},{3,4},{4,5},{5,6},{6,7},{7,8},{8,9},{9,10},{10,1... | collective-permute-start | bytes 872 | tf_op jit(solution)/shard_map/ppermute | solution.py:20
  400.4 6.5 collective-permute-start.101
  426.3 7.4 %collective-permute-start.106 = (f32[3,6,10,1]{3,1,2,0:T(8,128)S(1)}, f32[3,6,10,1]{3,1,2,0:T(8,128)S(1)}, u32[]{:S(2)}, u32[]{:S(2)}) collective-permute-start(f32[3,6,10,1]{3,1,2,0:T(8,128)S(1)} %get-tuple-element.78), channel_id=1, source_target_pairs={{1,0},{2,1},{3,2},{4,3},{5,4},{6,5},{7,6},{8,7},{9,8},{10,9},{11,1... | collective-permute-start | bytes 2168 | tf_op jit(solution)/shard_map/ppermute | solution.py:21
  428.3 6.7 %collective-permute-start.107 = (f32[3,6,10,1]{3,1,2,0:T(8,128)S(1)}, f32[3,6,10,1]{3,1,2,0:T(8,128)S(1)}, u32[]{:S(2)}, u32[]{:S(2)}) collective-permute-start(f32[3,6,10,1]{3,1,2,0:T(8,128)S(1)} %get-tuple-element.79), channel_id=1, source_target_pairs={{0,1},{1,2},{2,3},{3,4},{4,5},{5,6},{6,7},{7,8},{8,9},{9,10},{10,1... | collective-permute-start | bytes 2168 | tf_op jit(solution)/shard_map/ppermute | solution.py:20
  450.3 8.9 %collective-permute-start.112 = (f32[3,6,10,1]{3,1,2,0:T(8,128)S(1)}, f32[3,6,10,1]{3,1,2,0:T(8,128)S(1)}, u32[]{:S(2)}, u32[]{:S(2)}) collective-permute-start(f32[3,6,10,1]{3,1,2,0:T(8,128)S(1)} %get-tuple-element.74), channel_id=1, source_target_pairs={{1,0},{2,1},{3,2},{4,3},{5,4},{6,5},{7,6},{8,7},{9,8},{10,9},{11,1... | collective-permute-start | bytes 2168 | tf_op jit(solution)/shard_map/ppermute | solution.py:21
  452.3 8.2 %collective-permute-start.113 = (f32[3,6,10,1]{3,1,2,0:T(8,128)S(1)}, f32[3,6,10,1]{3,1,2,0:T(8,128)S(1)}, u32[]{:S(2)}, u32[]{:S(2)}) collective-permute-start(f32[3,6,10,1]{3,1,2,0:T(8,128)S(1)} %get-tuple-element.75), channel_id=1, source_target_pairs={{0,1},{1,2},{2,3},{3,4},{4,5},{5,6},{6,7},{7,8},{8,9},{9,10},{10,1... | collective-permute-start | bytes 2168 | tf_op jit(solution)/shard_map/ppermute | solution.py:20
  476.5 10.5 %collective-permute-start.119 = (f32[3,10,18,1]{3,2,1,0:T(8,128)S(1)}, f32[3,10,18,1]{3,2,1,0:T(8,128)S(1)}, u32[]{:S(2)}, u32[]{:S(2)}) collective-permute-start(f32[3,10,18,1]{3,2,1,0:T(8,128)S(1)} %get-tuple-element.47), channel_id=1, source_target_pairs={{0,1},{1,2},{2,3},{3,4},{4,5},{5,6},{6,7},{7,8},{8,9},{9,10},{10,1... | collective-permute-start | bytes 6488 | tf_op jit(solution)/shard_map/ppermute | solution.py:20
  482.6 8.8 %collective-permute-start.118 = (f32[3,10,18,1]{3,2,1,0:T(8,128)S(1)}, f32[3,10,18,1]{3,2,1,0:T(8,128)S(1)}, u32[]{:S(2)}, u32[]{:S(2)}) collective-permute-start(f32[3,10,18,1]{3,2,1,0:T(8,128)S(1)} %get-tuple-element.46), channel_id=1, source_target_pairs={{1,0},{2,1},{3,2},{4,3},{5,4},{6,5},{7,6},{8,7},{9,8},{10,9},{11,1... | collective-permute-start | bytes 6488 | tf_op jit(solution)/shard_map/ppermute | solution.py:21
  491.8 6.2 collective-permute-start.120
  505.8 7.6 %collective-permute-start.125 = (f32[3,10,18,1]{3,2,1,0:T(8,128)S(1)}, f32[3,10,18,1]{3,2,1,0:T(8,128)S(1)}, u32[]{:S(2)}, u32[]{:S(2)}) collective-permute-start(f32[3,10,18,1]{3,2,1,0:T(8,128)S(1)} %get-tuple-element.45), channel_id=1, source_target_pairs={{0,1},{1,2},{2,3},{3,4},{4,5},{5,6},{6,7},{7,8},{8,9},{9,10},{10,1... | collective-permute-start | bytes 6488 | tf_op jit(solution)/shard_map/ppermute | solution.py:20
  509.0 9.6 %collective-permute-start.124 = (f32[3,10,18,1]{3,2,1,0:T(8,128)S(1)}, f32[3,10,18,1]{3,2,1,0:T(8,128)S(1)}, u32[]{:S(2)}, u32[]{:S(2)}) collective-permute-start(f32[3,10,18,1]{3,2,1,0:T(8,128)S(1)} %get-tuple-element.44), channel_id=1, source_target_pairs={{1,0},{2,1},{3,2},{4,3},{5,4},{6,5},{7,6},{8,7},{9,8},{10,9},{11,1... | collective-permute-start | bytes 6488 | tf_op jit(solution)/shard_map/ppermute | solution.py:21
  532.2 7.6 %collective-permute-start.131 = (f32[3,10,18,1]{3,2,1,0:T(8,128)S(1)}, f32[3,10,18,1]{3,2,1,0:T(8,128)S(1)}, u32[]{:S(2)}, u32[]{:S(2)}) collective-permute-start(f32[3,10,18,1]{3,2,1,0:T(8,128)S(1)} %get-tuple-element.43), channel_id=1, source_target_pairs={{0,1},{1,2},{2,3},{3,4},{4,5},{5,6},{6,7},{7,8},{8,9},{9,10},{10,1... | collective-permute-start | bytes 6488 | tf_op jit(solution)/shard_map/ppermute | solution.py:20
  535.4 9.4 %collective-permute-start.130 = (f32[3,10,18,1]{3,2,1,0:T(8,128)S(1)}, f32[3,10,18,1]{3,2,1,0:T(8,128)S(1)}, u32[]{:S(2)}, u32[]{:S(2)}) collective-permute-start(f32[3,10,18,1]{3,2,1,0:T(8,128)S(1)} %get-tuple-element.42), channel_id=1, source_target_pairs={{1,0},{2,1},{3,2},{4,3},{5,4},{6,5},{7,6},{8,7},{9,8},{10,9},{11,1... | collective-permute-start | bytes 6488 | tf_op jit(solution)/shard_map/ppermute | solution.py:21
  (71 other events, 554.6 us)
where the time goes:
time: 674 us; the launch traced here: 670 us
  starting transfers between devices  394 us (58%)
  blocking collectives  124 us (18%)
  waiting for transfers between devices  100 us (15%)
  local copies, waits for them, and re-layouts  27.5 us (4%)
  other arithmetic  21.6 us (3%)
    ppermute x66, starting transfers between devices, padded_2(): before = lax.ppermute(last, axis, up)  289 us
    psum x1, blocking collectives, body(): summed = lax.psum(partial_sums, ('row', 'col', 'dep'))  124 us
    ppermute x66, starting transfers between devices, padded_2(): after = lax.ppermute(first, axis, down)  104 us
    ppermute x66, waiting for transfers between devices, padded_2(): after = lax.ppermute(first, axis, down)  62.8 us
    ppermute x66, waiting for transfers between devices, padded_2(): before = lax.ppermute(last, axis, up)  37.3 us
    reshape x3, local copies, waits for them, and re-layouts, coarsen(): field.reshape(leading + (size_x // 2, 2, size_y // 2, 2, size_z // 2, 2))  21.1 us
  transfers between devices with their start and end apart: 132, of which 57 were waited for; matrix products, arithmetic and copies ran while one was open for 2% of the time, Pallas kernels for 0%

commit v1 on v0

v1 whole, which is shorter than its diff:
```python
import jax
import jax.numpy as jnp
from jax import lax
from jax.experimental import pallas as pl
from jax.experimental.pallas import tpu as pltpu
from jax.sharding import PartitionSpec as P


RELAX = 0.8
LANES = 128
PAD = 8
HALO0 = 4
HALO1 = 40
OWN0 = 128
OWN1 = 64
NZ0 = OWN0 + 2 * HALO0
NZ1 = OWN1 + 2 * HALO1
NZ2 = NZ1 // 2
NZ3 = 40
VMEM_LIMIT = 56 * 1024 * 1024


def lanes_of(shape=(8, LANES)):
    return lax.broadcasted_iota(jnp.int32, shape, 1)


def turned(tile, amount):
    return pltpu.roll(tile, amount % LANES, 1)


def harmonic(a, b):
    return 2.0 * a * b / jnp.maximum(a + b, 1e-30)


def tiles(count):
    return range(0, count, 8)


def zero_pads(ref, lead, nz):
    zero = jnp.zeros((8, LANES), jnp.float32)
    for idx in lead:
        ref[(*idx, pl.ds(0, 8), slice(None))] = zero
        ref[(*idx, pl.ds(PAD + nz, 8), slice(None))] = zero


def wrap_rows(ref, lead, nx, nz):
    for idx in lead:
        for t in tiles(nz):
            rows = pl.ds(PAD + t, 8)
            ref[(*idx, 0, rows, slice(None))] = turned(ref[(*idx, nx, rows, slice(None))], 64)
            ref[(*idx, nx + 1, rows, slice(None))] = turned(ref[(*idx, 1, rows, slice(None))], 64)


def coefficients(k, wx, wy, wz, emit, level, nx, nz):
    step = 1 << level
    lane = lanes_of()
    low_half = lane < 64
    y_first = (lane % 64) < step
    y_last = (lane % 64) >= 64 - step
    zero = jnp.zeros((8, LANES), jnp.float32)
    for t in tiles(nz):
        rows = pl.ds(PAD + t, 8)
        k[0, rows, :] = jnp.where(low_half, 0.0, turned(k[nx, rows, :], 64))
        k[nx + 1, rows, :] = jnp.where(low_half, turned(k[1, rows, :], 64), 0.0)

    def faces(x, carry):
        wz[x, pl.ds(0, 8), :] = zero
        for t in tiles(nz):
            rows = pl.ds(PAD + t, 8)
            kc = k[x + 1, rows, :]
            wx[x + 1, rows, :] = harmonic(kc, k[x + 2, rows, :])
            wy[x, rows, :] = harmonic(kc, jnp.where(y_last, 0.0, turned(kc, -step)))
            wz[x, rows, :] = harmonic(kc, k[x + 1, pl.ds(PAD + t + 1, 8), :])
        return carry

    lax.fori_loop(0, nx, faces, 0)
    for t in tiles(nz):
        rows = pl.ds(PAD + t, 8)
        wx[0, rows, :] = turned(wx[nx, rows, :], 64)

    def cells(x, carry):
        for t in tiles(nz):
            rows = pl.ds(PAD + t, 8)
            kc = k[x + 1, rows, :]
            wyp = wy[x, rows, :]
            weights = [
                wx[x + 1, rows, :],
                wx[x, rows, :],
                wyp,
                turned(wyp, step),
                wz[x, rows, :],
                wz[x, pl.ds(PAD + t - 1, 8), :],
            ]
            outer = [
                k[x + 2, rows, :] == 0.0,
                k[x, rows, :] == 0.0,
                y_last,
                y_first,
                k[x + 1, pl.ds(PAD + t + 1, 8), :] == 0.0,
                k[x + 1, pl.ds(PAD + t - 1, 8), :] == 0.0,
            ]
            full = [jnp.where(o, kc, w) for o, w in zip(outer, weights)]
            total = full[0]
            for w in full[1:]:
                total = total + w
            total = jnp.where(kc > 0.0, total, 1.0)
            emit(x, t, kc, outer, weights, full, total)
        return carry

    lax.fori_loop(0, nx, cells, 0)


def neighbours(c, v, x, c0, v0row, step):
    coef = [c[n, x, pl.ds(c0, 8), :] for n in range(6)]
    centres, sums = [], []
    for f in range(3):
        vc = v[f, x + 1, pl.ds(v0row, 8), :]
        acc = coef[0] * v[f, x + 2, pl.ds(v0row, 8), :] + coef[1] * v[f, x, pl.ds(v0row, 8), :]
        acc = acc + (coef[2] * turned(vc, -step) + coef[3] * turned(vc, step))
        acc = acc + (
            coef[4] * v[f, x + 1, pl.ds(v0row + 1, 8), :] + coef[5] * v[f, x + 1, pl.ds(v0row - 1, 8), :]
        )
        centres.append(vc)
        sums.append(acc)
    return centres, sums


def sweep(c, v, first, out, level, nx, lo, hi):
    step = 1 << level

    def row(x, carry):
        for t in range(lo, hi, 8):
            centres, sums = neighbours(c, v, x, t, PAD + t, step)
            for f in range(3):
                out[f, x + 1, pl.ds(PAD + t, 8), :] = sums[f] + (
                    first[f, x, pl.ds(t, 8), :] + (1.0 - RELAX) * centres[f]
                )
        return carry

    lax.fori_loop(0, nx, row, 0)
    wrap_fields(out, nx, lo, hi)


def wrap_fields(v, nx, lo, hi):
    for f in range(3):
        for t in range(lo, hi, 8):
            rows = pl.ds(PAD + t, 8)
            v[f, 0, rows, :] = turned(v[f, nx, rows, :], 64)
            v[f, nx + 1, rows, :] = turned(v[f, 1, rows, :], 64)


def residual(c, v, first, invq, r, level, nx, nz):
    step = 1 << level

    def row(x, carry):
        for t in tiles(nz):
            centres, sums = neighbours(c, v, x, t, PAD + t, step)
            scale = invq[x, pl.ds(t, 8), :]
            for f in range(3):
                r[f, x, pl.ds(t, 8), :] = (
                    sums[f] + (first[f, x, pl.ds(t, 8), :] - RELAX * centres[f])
                ) * scale
        return carry

    lax.fori_loop(0, nx, row, 0)


def mean8(read, level):
    step = 1 << level
    total = (read(0, 0) + read(0, 1)) + (read(1, 0) + read(1, 1))
    upper = (lanes_of() // step) % 2 == 1
    mate = jnp.where(upper, turned(total, step), turned(total, -step))
    return (total + mate) * 0.125


def strided(start):
    return pl.ds(start, 8, stride=2)


def look_up(labels_ref, table_ref, out_ref):
    labels = labels_ref[...]
    k = jnp.zeros(labels.shape, jnp.float32)
    for phase in range(8):
        k = jnp.where(labels == phase, table_ref[phase], k)
    out_ref[...] = k.reshape(LANES, LANES).T


def down_kernel(blocks, c, v0, v1, g, own, low, high, diag, k, wx, wy, wz, invq, r, va, vb):
    lane = lanes_of()

    def place(t, carry):
        rows = pl.ds(pl.multiple_of(t * 8, 8), 8)
        for odd in range(2):
            held = [blocks[(2 * (g8 // 4) + odd) * 4 + g8 % 4, rows, :] for g8 in range(8)]
            for bit in range(3):
                dist = 1 << bit
                clear = (lane // (16 * dist)) % 2 == 0
                for i in range(8):
                    if not i & dist:
                        a, b = held[i], held[i + dist]
                        held[i] = jnp.where(clear, a, turned(b, 16 * dist))
                        held[i + dist] = jnp.where(clear, turned(a, -16 * dist), b)
            for x8 in range(8):
                k[odd * 8 + x8 + 1, pl.ds(pl.multiple_of(PAD + t * 8, 8), 8), :] = held[x8]
        return carry

    lax.fori_loop(0, NZ0 // 8, place, 0)
    zero_pads(k, [(x,) for x in range(18)], NZ0)
    zero_pads(va, [(f, x) for f in range(3) for x in range(18)], NZ0)
    zero_pads(vb, [(f, x) for f in range(3) for x in range(18)], NZ0)

    diag[...] = jnp.zeros_like(diag)
    zeros = jnp.zeros((8, LANES), jnp.float32)

    def emit(x, t, kc, outer, weights, full, total):
        rows = pl.ds(t, 8)
        q = RELAX / total
        for n in range(6):
            c[n, x, rows, :] = q * weights[n]
        invq[x, rows, :] = (1.0 / RELAX) * total
        depth = lax.broadcasted_iota(jnp.int32, (8, LANES), 0) + (t - HALO0)
        inside = (depth >= 0) & (depth < OWN0)
        for f in range(3):
            up, down = full[2 * f], full[2 * f + 1]
            first = q * (down - up)
            v0[f, x, rows, :] = first
            va[f, x + 1, pl.ds(PAD + t, 8), :] = first
            half_up = jnp.where(outer[2 * f], 0.5 * up, up)
            half_down = jnp.where(outer[2 * f + 1], 0.5 * down, down)
            g[f, x, rows, :] = half_down - half_up
            diag[f, :, :] = diag[f, :, :] + jnp.where(inside, 0.5 * (up + down), 0.0)

    coefficients(k, wx, wy, wz, emit, 0, 16, NZ0)
    wrap_fields(va, 16, 0, NZ0)
    sweep(c, va, v0, vb, 0, 16, 0, NZ0)
    residual(c, vb, v0, invq, r, 0, 16, NZ0)

    def save(x, carry):
        for f in range(3):
            for t in tiles(NZ0):
                v1[f, x, pl.ds(t, 8), :] = vb[f, x + 1, pl.ds(PAD + t, 8), :]
        return carry

    lax.fori_loop(0, 16, save, 0)

    def coarse(x, carry):
        for t in tiles(OWN1):
            for f in range(3):
                own[f, x, pl.ds(t, 8), :] = mean8(
                    lambda dx, dz: r[f, 2 * x + dx, strided(HALO0 + 2 * t + dz), :], 0
                )
            own[3, x, pl.ds(t, 8), :] = mean8(
                lambda dx, dz: k[2 * x + dx + 1, strided(PAD + HALO0 + 2 * t + dz), :], 0
            )
        even = lane % 2 == 0
        for ref, base in ((low, 0), (high, OWN1 - HALO1)):
            for t in tiles(HALO1):
                rows = pl.ds(base + t, 8)
                for pair in range(2):
                    ref[pair, x, pl.ds(t, 8), :] = jnp.where(
                        even, own[2 * pair, x, rows, :], own[2 * pair + 1, x, rows, :]
                    )
        return carry

    lax.fori_loop(0, 8, coarse, 0)


def up_kernel(
    where_ref, c0, v00, v01, g, own, below, above, diag,
    p, sums,
    k1, wx1, wy1, wz1, c1, f1, q1, r1, va1, vb1,
    k2, wx2, wy2, wz2, c2, f2, q2, r2, va2, vb2,
    k3, wx3, wy3, wz3, c3, f3, va3, vb3,
    wide1, wide2, wide3, va0, vb0, acc,
):
    lane = lanes_of()
    even = lane % 2 == 0

    def fill(x, carry):
        for t in tiles(OWN1):
            for f in range(3):
                f1[f, x, pl.ds(HALO1 + t, 8), :] = own[f, x, pl.ds(t, 8), :]
            k1[x + 1, pl.ds(PAD + HALO1 + t, 8), :] = own[3, x, pl.ds(t, 8), :]
        for ref, base in ((below, 0), (above, HALO1 + OWN1)):
            for t in tiles(HALO1):
                for pair in range(2):
                    packed = ref[pair, x, pl.ds(t, 8), :]
                    one = jnp.where(even, packed, turned(packed, 1))
                    two = jnp.where(even, turned(packed, -1), packed)
                    f1[2 * pair, x, pl.ds(base + t, 8), :] = one
                    if pair == 0:
                        f1[1, x, pl.ds(base + t, 8), :] = two
                    else:
                        k1[x + 1, pl.ds(PAD + base + t, 8), :] = two
        return carry

    lax.fori_loop(0, 8, fill, 0)

    def prepare(level, nx, nz, k, wx, wy, wz, c, first, invq, va, vb):
        zero_pads(k, [(x,) for x in range(nx + 2)], nz)
        zero_pads(va, [(f, x) for f in range(3) for x in range(nx + 2)], nz)
        zero_pads(vb, [(f, x) for f in range(3) for x in range(nx + 2)], nz)
        scale = 4.0**level

        def emit(x, t, kc, outer, weights, full, total):
            rows = pl.ds(t, 8)
            q = RELAX / total
            for n in range(6):
                c[n, x, rows, :] = q * weights[n]
            if invq is not None:
                invq[x, rows, :] = (1.0 / (RELAX * scale)) * total
            for f in range(3):
                start = (q * scale) * first[f, x, rows, :]
                first[f, x, rows, :] = start
                va[f, x + 1, pl.ds(PAD + t, 8), :] = start

        coefficients(k, wx, wy, wz, emit, level, nx, nz)
        wrap_fields(va, nx, 0, nz)

    def restrict(level, nx, nz, r, k, first, knext):
        def row(x, carry):
            for t in tiles(nz):
                for f in range(3):
                    first[f, x, pl.ds(t, 8), :] = mean8(
                        lambda dx, dz: r[f, 2 * x + dx, strided(2 * t + dz), :], level
                    )
                knext[x + 1, pl.ds(PAD + t, 8), :] = mean8(
                    lambda dx, dz: k[2 * x + dx + 1, strided(PAD + 2 * t + dz), :], level
                )
            return carry

        lax.fori_loop(0, nx, row, 0)

    def widen(e, wide, nx, first_row, count):
        def row(x, carry):
            for f in range(3):
                for t in tiles(count):
                    part = e[f, x + 1, pl.ds(PAD + first_row + t, 8), :]
                    wide[f, x, strided(2 * t), :] = part
                    wide[f, x, strided(2 * t + 1), :] = part
            return carry

        lax.fori_loop(0, nx, row, 0)

    def add_coarse(v, wide, nx, lo, hi, first_row):
        def row(x, carry):
            for f in range(3):
                for t in range(lo, hi, 8):
                    rows = pl.ds(PAD + t, 8)
                    v[f, x + 1, rows, :] = v[f, x + 1, rows, :] + wide[f, x // 2, pl.ds(t - first_row, 8), :]
            return carry

        lax.fori_loop(0, nx, row, 0)
        wrap_fields(v, nx, lo, hi)

    prepare(1, 8, NZ1, k1, wx1, wy1, wz1, c1, f1, q1, va1, vb1)
    sweep(c1, va1, f1, vb1, 1, 8, 0, NZ1)
    residual(c1, vb1, f1, q1, r1, 1, 8, NZ1)
    restrict(1, 4, NZ2, r1, k1, f2, k2)

    prepare(2, 4, NZ2, k2, wx2, wy2, wz2, c2, f2, q2, va2, vb2)
    sweep(c2, va2, f2, vb2, 2, 4, 0, NZ2)
    for f in range(3):
        for x in range(4):
            r2[f, x, pl.ds(NZ2, 8), :] = jnp.zeros((8, LANES), jnp.float32)
    residual(c2, vb2, f2, q2, r2, 2, 4, NZ2)
    restrict(2, 2, NZ3, r2, k2, f3, k3)

    prepare(3, 2, NZ3, k3, wx3, wy3, wz3, c3, f3, None, va3, vb3)
    sweep(c3, va3, f3, vb3, 3, 2, 0, NZ3)
    sweep(c3, vb3, f3, va3, 3, 2, 0, NZ3)
    sweep(c3, va3, f3, vb3, 3, 2, 0, NZ3)
    sweep(c3, vb3, f3, va3, 3, 2, 0, NZ3)
    sweep(c3, va3, f3, vb3, 3, 2, 0, NZ3)

    widen(vb3, wide3, 2, 0, NZ3)
    add_coarse(vb2, wide3, 4, 0, NZ2, 0)
    sweep(c2, vb2, f2, va2, 2, 4, 0, NZ2)
    sweep(c2, va2, f2, vb2, 2, 4, 0, NZ2)

    lo1, hi1 = HALO1 - 8, HALO1 + OWN1 + 8
    widen(vb2, wide2, 4, lo1 // 2, (hi1 - lo1) // 2)
    add_coarse(vb1, wide2, 8, lo1, hi1, lo1)
    sweep(c1, vb1, f1, va1, 1, 8, lo1, hi1)
    sweep(c1, va1, f1, vb1, 1, 8, lo1, hi1)

    widen(vb1, wide1, 8, HALO1 - HALO0 // 2, 72)
    zero_pads(va0, [(f, x) for f in range(3) for x in range(18)], NZ0)
    zero_pads(vb0, [(f, x) for f in range(3) for x in range(18)], NZ0)

    def add_first(x, carry):
        for f in range(3):
            for t in tiles(NZ0):
                va0[f, x + 1, pl.ds(PAD + t, 8), :] = (
                    v01[f, x, pl.ds(t, 8), :] + wide1[f, x // 2, pl.ds(t, 8), :]
                )
        return carry

    lax.fori_loop(0, 16, add_first, 0)
    wrap_fields(va0, 16, 0, NZ0)
    sweep(c0, va0, v00, vb0, 0, 16, 0, NZ0)

    acc[...] = jnp.zeros_like(acc)

    def last(x, carry):
        for t in tiles(OWN0):
            centres, near = neighbours(c0, vb0, x, HALO0 + t, PAD + HALO0 + t, 1)
            rows = pl.ds(HALO0 + t, 8)
            done = [
                near[f] + (v00[f, x, rows, :] + (1.0 - RELAX) * centres[f]) for f in range(3)
            ]
            for f in range(3):
                va0[f, x, pl.ds(t, 8), :] = done[f]
            for i in range(3):
                gi = g[i, x, rows, :]
                for j in range(3):
                    acc[3 * i + j, :, :] = acc[3 * i + j, :, :] + gi * done[j]
        return carry

    lax.fori_loop(0, 16, last, 0)

    flat = jnp.zeros((1, LANES), jnp.float32)
    one_row = lax.broadcasted_iota(jnp.int32, (1, LANES), 1)
    for i in range(3):
        for j in range(3):
            part = acc[3 * i + j, :, :]
            if i == j:
                part = part + diag[i, :, :]
            whole = jnp.sum(jnp.sum(part, axis=0, keepdims=True), axis=1, keepdims=True)
            flat = jnp.where(one_row == 3 * i + j, whole, flat)
    sums[...] = flat

    row_no, col_no = where_ref[0], where_ref[1]
    x_base = (row_no % 2) * 8
    lane_base = (row_no // 2) * 64 + col_no * 16
    wide_lane = lanes_of((OWN0, LANES))
    for f in range(3):
        block = jnp.zeros((OWN0, LANES), jnp.float32)
        for x8 in range(8):
            piece = va0[f, x_base + x8, pl.ds(0, OWN0), :]
            amount = lax.rem(x8 * 16 - lane_base + 2 * LANES, LANES)
            block = jnp.where(wide_lane // 16 == x8, pltpu.roll(piece, amount, 1), block)
        p[f, :, :] = block.T


def f32(*shape):
    return jax.ShapeDtypeStruct(shape, jnp.float32)


def scratch(*shape):
    return pltpu.VMEM(shape, jnp.float32)


def level_scratch(nx, nz, last=False):
    rows = nz + 2 * PAD
    got = [
        scratch(nx + 2, rows, LANES), scratch(nx + 1, rows, LANES), scratch(nx, rows, LANES),
        scratch(nx, rows, LANES), scratch(6, nx, nz, LANES), scratch(3, nx, nz, LANES),
    ]
    if not last:
        got += [scratch(nx, nz, LANES), scratch(3, nx, nz + 8, LANES)]
    return got + [scratch(3, nx + 2, rows, LANES)] * 2


def params():
    return pltpu.CompilerParams(vmem_limit_bytes=VMEM_LIMIT)


VM = pl.BlockSpec(memory_space=pltpu.VMEM)
SM = pl.BlockSpec(memory_space=pltpu.SMEM)


def conductivities(labels, table):
    return pl.pallas_call(
        look_up, out_shape=f32(LANES, LANES), in_specs=[VM, SM], out_specs=VM, name="look_up"
    )(labels, table)


def down(blocks):
    rows = NZ0 + 2 * PAD
    return pl.pallas_call(
        down_kernel,
        out_shape=[
            f32(6, 16, NZ0, LANES), f32(3, 16, NZ0, LANES), f32(3, 16, NZ0, LANES),
            f32(3, 16, NZ0, LANES), f32(4, 8, OWN1, LANES), f32(2, 8, HALO1, LANES),
            f32(2, 8, HALO1, LANES), f32(3, 8, LANES),
        ],
        in_specs=[VM],
        out_specs=[VM] * 8,
        scratch_shapes=[
            scratch(18, rows, LANES), scratch(17, rows, LANES), scratch(16, rows, LANES),
            scratch(16, rows, LANES), scratch(16, NZ0, LANES), scratch(3, 16, NZ0, LANES),
            scratch(3, 18, rows, LANES), scratch(3, 18, rows, LANES),
        ],
        compiler_params=params(),
        name="down",
    )(blocks)


def up(place, c0, v00, v01, g, own, below, above, diag):
    rows = NZ0 + 2 * PAD
    return pl.pallas_call(
        up_kernel,
        out_shape=[f32(3, LANES, LANES), f32(1, LANES)],
        in_specs=[SM] + [VM] * 8,
        out_specs=[VM] * 2,
        scratch_shapes=level_scratch(8, NZ1) + level_scratch(4, NZ2) + level_scratch(2, NZ3, True)
        + [
            scratch(3, 8, 144, LANES), scratch(3, 4, 80, LANES), scratch(3, 2, 80, LANES),
            scratch(3, 18, rows, LANES), scratch(3, 18, rows, LANES), scratch(9, 8, LANES),
        ],
        compiler_params=params(),
        name="up",
    )(place, c0, v00, v01, g, own, below, above, diag)


def from_below(x):
    n = lax.axis_size("dep")
    return lax.ppermute(x, "dep", [(i, i + 1) for i in range(n - 1)])


def from_above(x):
    n = lax.axis_size("dep")
    return lax.ppermute(x, "dep", [(i + 1, i) for i in range(n - 1)])


def body(labels, conductivity):
    k = conductivities(labels, conductivity)
    lower = from_below(k[OWN0 - HALO0 :])
    upper = from_above(k[:HALO0])
    column = jnp.concatenate([lower, k, upper], axis=0)
    plane = lax.axis_size("row") * lax.axis_size("col")
    blocks = lax.all_to_all(
        jnp.broadcast_to(column[None], (plane,) + column.shape), ("row", "col"), 0, 0
    )
    c0, v00, v01, g, own, low, high, diag = down(blocks)
    below = from_below(high)
    above = from_above(low)
    place = jnp.stack([lax.axis_index("row"), lax.axis_index("col")]).astype(jnp.int32)
    p, sums = up(place, c0, v00, v01, g, own, below, above, diag)
    depth = lax.axis_size("dep")
    parts = lax.all_to_all(jnp.broadcast_to(sums[None], (depth, 1, LANES)), "dep", 0, 0)
    cells = plane * labels.size * depth
    tensor = jnp.sum(parts, axis=(0, 1))[:9].reshape(3, 3) / cells
    return p.reshape((3,) + labels.shape), tensor


def solution(mesh):
    in_specs = (P("row", "col", "dep"), P())
    out_specs = (P(None, "row", "col", "dep"), P())
    return jax.shard_map(body, mesh=mesh, in_specs=in_specs, out_specs=out_specs, check_vma=False)
```

time: 674 us -> 136 us (0.20)
  starting transfers between devices: 394 us -> 15.6 us
  waiting for transfers between devices: 100 us -> 6.84 us
  blocking collectives: 124 us -> 50.2 us
  Pallas kernels: 0 us -> 57.4 us
  local copies, waits for them, and re-layouts: 27.5 us -> 2.84 us
  other arithmetic: 21.6 us -> 1.49 us
    ppermute x132 -> x4, starting transfers between devices: 394 us -> 15.6 us  [the longest x2 8.57 us: from_below(): return lax.ppermute(x, 'dep', [(i, i + 1) for i in range(n - 1)])]
    psum x1 -> x0, blocking collectives: 124 us -> none  [body(): summed = lax.psum(partial_sums, ('row', 'col', 'dep'))]
    ppermute x132 -> x4, waiting for transfers between devices: 100 us -> 6.84 us  [the longest x2 5.08 us: from_above(): return lax.ppermute(x, 'dep', [(i + 1, i) for i in range(n - 1)])]
    pallas_call x0 -> x3, Pallas kernels: none -> 57.4 us  [the longest x1 31.7 us: up(): pl.pallas_call(up_kernel, out_shape=[f32(3, LANES, LANES), f32(1, LANES)]...]
    all_to_all x0 -> x2, blocking collectives: none -> 50.2 us  [the longest x1 27.6 us: body(): lax.all_to_all(jnp.broadcast_to(sums[None], (depth, 1, LANES)), 'dep', 0, 0)]
    reshape x7 -> x0, local copies, waits for them, and re-layouts: 22.1 us -> none  [the longest x3 21.1 us: coarsen(): field.reshape(leading + (size_x // 2, 2, size_y // 2, 2, size_z // 2, 2))]
    add x21 -> x0, other arithmetic: 9.45 us -> none  [the longest x1 5.76 us: body(): cell_conduct + jnp.where(labels == phase, conductivity[phase], 0.0)]
    reduce_sum x10 -> x1, other arithmetic: 9.35 us -> 0.02 us  [body(): tensor = jnp.sum(parts, axis=(0, 1))[:9].reshape(3, 3) / cells]
  transfers between devices with their start and end apart: 132 -> 4, of which waited for: 57 -> 3; matrix products, arithmetic and copies ran while one was open for 2% -> 0% of each run, Pallas kernels for 0% -> 0%
where the time goes in v1:
time: 136 us; the launch traced here: 135 us
  Pallas kernels  57.4 us (42%)
  blocking collectives  50.2 us (37%)
  starting transfers between devices  15.6 us (11%)
  waiting for transfers between devices  6.84 us (5%)
  local copies, waits for them, and re-layouts  2.84 us (2%)
  other arithmetic  1.49 us (1%)
    pallas_call x1, Pallas kernels, up(): pl.pallas_call(up_kernel, out_shape=[f32(3, LANES, LANES), f32(1, LANES)]...  31.7 us
    all_to_all x1, blocking collectives, body(): lax.all_to_all(jnp.broadcast_to(sums[None], (depth, 1, LANES)), 'dep', 0, 0)  27.6 us
    pallas_call x1, Pallas kernels, down(): pl.pallas_call(down_kernel, out_shape=[f32(6, 16, NZ0, LANES), f32(3, 16,...  24.2 us
    all_to_all x1, blocking collectives, body(): lax.all_to_all(jnp.broadcast_to(column[None], (plane,) + column.shape), (...  22.6 us
    ppermute x2, starting transfers between devices, from_below(): return lax.ppermute(x, 'dep', [(i, i + 1) for i in range(n - 1)])  8.57 us
    ppermute x2, starting transfers between devices, from_above(): return lax.ppermute(x, 'dep', [(i + 1, i) for i in range(n - 1)])  7.06 us
    ppermute x2, waiting for transfers between devices, from_above(): return lax.ppermute(x, 'dep', [(i + 1, i) for i in range(n - 1)])  5.08 us
  transfers between devices with their start and end apart: 4, of which 3 were waited for; matrix products, arithmetic and copies ran while one was open for 0% of the time, Pallas kernels for 0%

profile of v1, /device:TPU:1, one launch (start us, length us, event | category | flops | bytes accessed | tf_op | source)
XLA Modules:
  0.0 135.1 jit_solution(18317944870237665568)
XLA Ops:
  0.6 1.6 %look_up.1 = f32[128,128]{1,0:T(8,128)} custom-call(s32[8,16,128]{2,1,0:T(8,128)} %labels_ref.1, f32[8]{0:T(128)} %table_ref.1), custom_call_target="tpu_custom_call" | custom-call | tf_op jit(solution)/shard_map/look_up/pallas_call | solution.py:474
  2.2 0.7 fusion
  2.9 4.9 %collective-permute-start = (f32[4,128]{1,0:T(4,128)S(1)}, f32[4,128]{1,0:T(4,128)S(1)}, u32[]{:S(2)}, u32[]{:S(2)}) collective-permute-start(f32[4,128]{1,0:T(4,128)S(1)} %get-tuple-element.22), channel_id=1, source_target_pairs={{0,1},{1,2},{2,3},{3,4},{4,5},{5,6},{6,7},{7,8},{8,9},{9,10},{10,1... | collective-permute-start | bytes 6152 | tf_op jit(solution)/shard_map/ppermute | solution.py:519
  7.9 5.1 %collective-permute-start.1 = (f32[4,128]{1,0:T(4,128)S(1)}, f32[4,128]{1,0:T(4,128)S(1)}, u32[]{:S(2)}, u32[]{:S(2)}) collective-permute-start(f32[4,128]{1,0:T(4,128)S(1)} %get-tuple-element.23), channel_id=1, source_target_pairs={{1,0},{2,1},{3,2},{4,3},{5,4},{6,5},{7,6},{8,7},{9,8},{10,9},{11,1... | collective-permute-start | bytes 6152 | tf_op jit(solution)/shard_map/ppermute | solution.py:524
  13.0 0.0 collective-permute-done
  13.0 0.8 collective-permute-done.1
  13.8 0.8 pad_maximum_fusion
  14.7 0.1 broadcast_in_dim.6
  14.7 22.6 %all_to_all.10.blocks = f32[16,136,128]{2,1,0:T(8,128)} all-to-all(f32[16,136,128]{2,1,0:T(8,128)S(1)} %broadcast_in_dim.6), channel_id=1, replica_groups=mesh['row'=4,'col'=4,'dep'=32] {'row','col'}, dimensions={0} | all-to-all | bytes 2228224 | tf_op jit(solution)/shard_map/all_to_all | solution.py:533
  37.3 24.2 %down.1 = (f32[6,16,136,128]{3,2,1,0:T(8,128)}, f32[3,16,136,128]{3,2,1,0:T(8,128)}, f32[3,16,136,128]{3,2,1,0:T(8,128)}, f32[3,16,136,128]{3,2,1,0:T(8,128)}, f...) custom-call(f32[16,136,128]{2,1,0:T(8,128)} %all_to_all.10.blocks), custom_call_target="tpu_custom_call" | custom-call | tf_op jit(solution)/shard_map/down/pallas_call | solution.py:481
  61.5 3.6 %collective-permute-start.2 = (f32[2,8,40,128]{3,2,1,0:T(8,128)}, f32[2,8,40,128]{3,2,1,0:T(8,128)S(1)}, u32[]{:S(2)}, u32[]{:S(2)}) collective-permute-start(f32[2,8,40,128]{3,2,1,0:T(8,128)} %get-tuple-element.17), channel_id=1, source_target_pairs={{0,1},{1,2},{2,3},{3,4},{4,5},{5,6},{6,7},{7,8},{8,9},{9,10},{10,1... | collective-permute-start | bytes 983048 | tf_op jit(solution)/shard_map/ppermute | solution.py:519
  65.2 1.9 %collective-permute-start.3 = (f32[2,8,40,128]{3,2,1,0:T(8,128)}, f32[2,8,40,128]{3,2,1,0:T(8,128)S(1)}, u32[]{:S(2)}, u32[]{:S(2)}) collective-permute-start(f32[2,8,40,128]{3,2,1,0:T(8,128)} %get-tuple-element.18), channel_id=1, source_target_pairs={{1,0},{2,1},{3,2},{4,3},{5,4},{6,5},{7,6},{8,7},{9,8},{10,9},{11,1... | collective-permute-start | bytes 983048 | tf_op jit(solution)/shard_map/ppermute | solution.py:524
  67.1 0.6 pad_add_fusion.where_ref
  67.7 1.8 %collective-permute-done.2.below = f32[2,8,40,128]{3,2,1,0:T(8,128)S(1)} collective-permute-done((f32[2,8,40,128]{3,2,1,0:T(8,128)}, f32[2,8,40,128]{3,2,1,0:T(8,128)S(1)}, u32[]{:S(2)}, u32[]{:S(2)}) %collective-permute-start.2) | collective-permute-done | bytes 327712 | tf_op jit(solution)/shard_map/ppermute | solution.py:519
  69.5 0.0 copy-start
  69.5 4.3 %collective-permute-done.3.above = f32[2,8,40,128]{3,2,1,0:T(8,128)S(1)} collective-permute-done((f32[2,8,40,128]{3,2,1,0:T(8,128)}, f32[2,8,40,128]{3,2,1,0:T(8,128)S(1)}, u32[]{:S(2)}, u32[]{:S(2)}) %collective-permute-start.3) | collective-permute-done | bytes 327712 | tf_op jit(solution)/shard_map/ppermute | solution.py:524
  73.8 0.0 copy-start.1
  73.8 0.0 copy-done
  73.8 0.7 copy-done.1
  74.5 31.7 %up.1 = (f32[3,128,128]{2,1,0:T(8,128)}, f32[1,128]{1,0:T(1,128)}) custom-call(s32[2]{0:T(128)} %pad_add_fusion.where_ref, f32[6,16,136,128]{3,2,1,0:T(8,128)} %get-tuple-element.12.c0, f32[3,16,136,128]{3,2,1,0:T(8,128)} %get-tuple-element.13.v00, f32[3,16,136,128]{3,2,1,0:T(8,128)} %get-tuple-element.14.v01, f32[3,16,136,128]{3,2,1,0:T(8,128)} %get-tuple-element.15.g, ...), custom_call_target="tpu_custom_call" | custom-call | tf_op jit(solution)/shard_map/up/pallas_call | solution.py:502
  106.2 0.7 broadcast_in_dim.16
  106.8 27.6 %all_to_all.11 = f32[32,1,128]{2,1,0:T(1,128)S(1)} all-to-all(f32[32,1,128]{2,1,0:T(1,128)S(1)} %broadcast_in_dim.16), channel_id=1, replica_groups=mesh['row'=4,'col'=4,'dep'=32] {'dep'}, dimensions={0} | all-to-all | bytes 32768 | tf_op jit(solution)/shard_map/all_to_all | solution.py:542
  134.4 0.7 div.6
  (2 shorter events, 0.0 us)
Async XLA Ops:
  2.9 10.1 %collective-permute-start = (f32[4,128]{1,0:T(4,128)S(1)}, f32[4,128]{1,0:T(4,128)S(1)}, u32[]{:S(2)}, u32[]{:S(2)}) collective-permute-start(f32[4,128]{1,0:T(4,128)S(1)} %get-tuple-element.22), channel_id=1, source_target_pairs={{0,1},{1,2},{2,3},{3,4},{4,5},{5,6},{6,7},{7,8},{8,9},{9,10},{10,1... | collective-permute-start | bytes 6152 | tf_op jit(solution)/shard_map/ppermute | solution.py:519
  7.9 5.9 %collective-permute-start.1 = (f32[4,128]{1,0:T(4,128)S(1)}, f32[4,128]{1,0:T(4,128)S(1)}, u32[]{:S(2)}, u32[]{:S(2)}) collective-permute-start(f32[4,128]{1,0:T(4,128)S(1)} %get-tuple-element.23), channel_id=1, source_target_pairs={{1,0},{2,1},{3,2},{4,3},{5,4},{6,5},{7,6},{8,7},{9,8},{10,9},{11,1... | collective-permute-start | bytes 6152 | tf_op jit(solution)/shard_map/ppermute | solution.py:524
  61.5 8.0 %collective-permute-start.2 = (f32[2,8,40,128]{3,2,1,0:T(8,128)}, f32[2,8,40,128]{3,2,1,0:T(8,128)S(1)}, u32[]{:S(2)}, u32[]{:S(2)}) collective-permute-start(f32[2,8,40,128]{3,2,1,0:T(8,128)} %get-tuple-element.17), channel_id=1, source_target_pairs={{0,1},{1,2},{2,3},{3,4},{4,5},{5,6},{6,7},{7,8},{8,9},{9,10},{10,1... | collective-permute-start | bytes 983048 | tf_op jit(solution)/shard_map/ppermute | solution.py:519
  65.2 8.6 %collective-permute-start.3 = (f32[2,8,40,128]{3,2,1,0:T(8,128)}, f32[2,8,40,128]{3,2,1,0:T(8,128)S(1)}, u32[]{:S(2)}, u32[]{:S(2)}) collective-permute-start(f32[2,8,40,128]{3,2,1,0:T(8,128)} %get-tuple-element.18), channel_id=1, source_target_pairs={{1,0},{2,1},{3,2},{4,3},{5,4},{6,5},{7,6},{8,7},{9,8},{10,9},{11,1... | collective-permute-start | bytes 983048 | tf_op jit(solution)/shard_map/ppermute | solution.py:524
  69.5 4.3 %copy-start = (f32[2,8,40,128]{3,2,1,0:T(8,128)}, f32[2,8,40,128]{3,2,1,0:T(8,128)S(1)}, u32[]{:S(2)}) copy-start(f32[2,8,40,128]{3,2,1,0:T(8,128)S(1)} %collective-permute-done.2.below) | copy-start | bytes 983044
  73.8 0.7 copy-start.1

commit v2 on v0

v2 whole, which is shorter than its diff:
```python
import jax
import jax.numpy as jnp
from jax import lax
from jax.experimental import pallas as pl
from jax.experimental.pallas import tpu as pltpu
from jax.sharding import PartitionSpec as P


RELAX = 0.8
LANES = 128
PAD = 8
HALO0 = 4
HALO1 = 40
OWN0 = 128
OWN1 = 64
NZ0 = OWN0 + 2 * HALO0
NZ1 = OWN1 + 2 * HALO1
NZ2 = NZ1 // 2
NZ3 = 40
VMEM_LIMIT = 56 * 1024 * 1024


def lanes_of(shape=(8, LANES)):
    return lax.broadcasted_iota(jnp.int32, shape, 1)


def turned(tile, amount):
    return pltpu.roll(tile, amount % LANES, 1)


def span(start):
    return pl.ds(start, 8)


def strided(start):
    return pl.ds(start, 8, stride=2)


def harmonic(a, b):
    return (2.0 * a) * b * pl.reciprocal(jnp.maximum(a + b, 1e-30))


def over(lo, hi, step, carry=0):
    if hi - lo <= 80:
        for t in range(lo, hi, 8):
            carry = step(t, carry)
        return carry
    return lax.fori_loop(
        0, (hi - lo) // 8, lambda i, held: step(pl.multiple_of(lo + 8 * i, 8), held), carry
    )


def zero_pads(ref, lead, nz):
    zero = jnp.zeros((8, LANES), jnp.float32)
    for idx in lead:
        ref[(*idx, span(0), slice(None))] = zero
        ref[(*idx, span(PAD + nz), slice(None))] = zero


def cells_of(side):
    return [(x, y) for x in range(side) for y in range(side)]


def fields_of(side):
    return [(f, x, y) for f in range(3) for x, y in cells_of(side)]


def strides_of(level):
    return (32, 2) if level == 3 else (16, 1)


class Edges:
    def __init__(self, level):
        xs, ys = strides_of(level)
        lane = lanes_of()
        self.x_first, self.x_last = lane < xs, lane >= LANES - xs
        self.y_first, self.y_last = (lane & 15) < ys, (lane & 15) >= 16 - ys


def beside(read, side, level, x, y):
    xs, ys = strides_of(level)
    last = side - 1
    return [
        read(x + 1, y) if x < last else turned(read(0, y), -xs),
        read(x - 1, y) if x > 0 else turned(read(last, y), xs),
        read(x, y + 1) if y < last else turned(read(x, 0), -ys),
        read(x, y - 1) if y > 0 else turned(read(x, last), ys),
    ]


def coefficients(k, wx, wy, wz, emit, level, side, nz, carry=0):
    xs, ys = strides_of(level)
    last = side - 1
    edges = Edges(level)
    zero = jnp.zeros((8, LANES), jnp.float32)
    for x, y in cells_of(side):
        wz[x, y, span(0), :] = zero

    def faces(t, held):
        rows = span(PAD + t)
        for x, y in cells_of(side):
            kc = k[x, y, rows, :]
            if x < last:
                kx = k[x + 1, y, rows, :]
            else:
                kx = jnp.where(edges.x_last, 0.0, turned(k[0, y, rows, :], -xs))
            if y < last:
                ky = k[x, y + 1, rows, :]
            else:
                ky = jnp.where(edges.y_last, 0.0, turned(k[x, 0, rows, :], -ys))
            wx[x, y, rows, :] = harmonic(kc, kx)
            wy[x, y, rows, :] = harmonic(kc, ky)
            wz[x, y, rows, :] = harmonic(kc, k[x, y, span(PAD + t + 1), :])
        return held

    over(0, nz, faces)

    def cells(t, held):
        rows = span(PAD + t)
        for x, y in cells_of(side):
            kc = k[x, y, rows, :]
            weights = [
                wx[x, y, rows, :],
                wx[x - 1, y, rows, :] if x > 0 else turned(wx[last, y, rows, :], xs),
                wy[x, y, rows, :],
                wy[x, y - 1, rows, :] if y > 0 else turned(wy[x, last, rows, :], ys),
                wz[x, y, rows, :],
                wz[x, y, span(PAD + t - 1), :],
            ]
            outer = [
                edges.x_last if x == last else None,
                edges.x_first if x == 0 else None,
                edges.y_last if y == last else None,
                edges.y_first if y == 0 else None,
                k[x, y, span(PAD + t + 1), :] == 0.0,
                k[x, y, span(PAD + t - 1), :] == 0.0,
            ]
            full = [w if o is None else jnp.where(o, kc, w) for o, w in zip(outer, weights)]
            total = full[0]
            for w in full[1:]:
                total = total + w
            total = jnp.where(kc > 0.0, total, 1.0)
            held = emit(t, held, x, y, outer, weights, full, total)
        return held

    return over(0, nz, cells, carry)


def neighbours(c, v, side, level, x, y, t):
    coef = [c[n, x, y, span(t), :] for n in range(6)]
    centres, sums = [], []
    for f in range(3):
        near = beside(lambda i, j: v[f, i, j, span(PAD + t), :], side, level, x, y)
        near += [v[f, x, y, span(PAD + t + 1), :], v[f, x, y, span(PAD + t - 1), :]]
        parts = [a * b for a, b in zip(coef, near)]
        centres.append(v[f, x, y, span(PAD + t), :])
        sums.append(((parts[0] + parts[1]) + (parts[2] + parts[3])) + (parts[4] + parts[5]))
    return centres, sums


def sweep(c, v, first, out, level, side, lo, hi):
    def step(t, held):
        for x, y in cells_of(side):
            centres, sums = neighbours(c, v, side, level, x, y, t)
            for f in range(3):
                out[f, x, y, span(PAD + t), :] = sums[f] + (
                    first[f, x, y, span(t), :] + (1.0 - RELAX) * centres[f]
                )
        return held

    over(lo, hi, step)


def residual(c, v, first, invq, r, level, side, nz):
    def step(t, held):
        for x, y in cells_of(side):
            centres, sums = neighbours(c, v, side, level, x, y, t)
            scale = invq[x, y, span(t), :]
            for f in range(3):
                r[f, x, y, span(t), :] = (
                    sums[f] + (first[f, x, y, span(t), :] - RELAX * centres[f])
                ) * scale
        return held

    over(0, nz, step)


def mean8(read, x, y):
    total = None
    for dx in range(2):
        for dy in range(2):
            part = read(2 * x + dx, 2 * y + dy, 0) + read(2 * x + dx, 2 * y + dy, 1)
            total = part if total is None else total + part
    return total * 0.125


def mean8_lanes(read):
    lane = lanes_of()
    total = read(0, 0, 0) + read(0, 0, 1)
    for stride in (16, 1):
        mate = jnp.where((lane & stride) != 0, turned(total, stride), turned(total, -stride))
        total = total + mate
    return total * 0.125


def look_up(labels_ref, table_ref, out_ref, high_ref, low_ref, mixed):
    for x in range(8):
        for ylo in range(4):
            labels = labels_ref[x, pl.ds(ylo, 4, stride=4), :]
            k = jnp.zeros(labels.shape, jnp.float32)
            for phase in range(8):
                k = jnp.where(labels == phase, table_ref[phase], k)
            mixed[pl.ds((x % 4) * 32 + (x // 4) * 16 + ylo * 4, 4), :] = k
    column = mixed[...].T
    out_ref[...] = column
    low_ref[...] = column[:HALO0]
    high_ref[...] = column[OWN0 - HALO0 :]


def down_kernel(
    blocks, c_out, v0_out, v1_out, g_out, own, diag, k, wx, wy, wz, c, v0, g, invq, r, va, vb, sems
):
    lane = lanes_of()
    zero_pads(k, cells_of(4), NZ0)
    zero_pads(va, fields_of(4), NZ0)
    zero_pads(vb, fields_of(4), NZ0)

    def place(t, held):
        tiles = [blocks[n, span(t), :] for n in range(16)]
        for bit, stride in ((0, 4), (1, 8), (2, 32), (3, 64)):
            dist = 1 << bit
            clear = (lane & stride) == 0
            for i in range(16):
                if not i & dist:
                    a, b = tiles[i], tiles[i + dist]
                    tiles[i] = jnp.where(clear, a, turned(b, stride))
                    tiles[i + dist] = jnp.where(clear, turned(a, -stride), b)
        for x, y in cells_of(4):
            k[x, y, span(PAD + t), :] = tiles[4 * x + y]
        return held

    over(0, NZ0, place)

    def emit(t, held, x, y, outer, weights, full, total):
        rows = span(t)
        q = RELAX * pl.reciprocal(total)
        for n in range(6):
            c[n, x, y, rows, :] = q * weights[n]
        invq[x, y, rows, :] = (1.0 / RELAX) * total
        depth = lax.broadcasted_iota(jnp.int32, (8, LANES), 0) + (t - HALO0)
        inside = (depth >= 0) & (depth < OWN0)
        held = list(held)
        for f in range(3):
            up, down = full[2 * f], full[2 * f + 1]
            first = q * (down - up)
            v0[f, x, y, rows, :] = first
            va[f, x, y, span(PAD + t), :] = first
            upper, lower = outer[2 * f], outer[2 * f + 1]
            half_up = up if upper is None else jnp.where(upper, 0.5 * up, up)
            half_down = down if lower is None else jnp.where(lower, 0.5 * down, down)
            g[f, x, y, rows, :] = half_down - half_up
            held[f] = held[f] + jnp.where(inside, up + down, 0.0)
        return tuple(held)

    nothing = jnp.zeros((8, LANES), jnp.float32)
    sides = coefficients(k, wx, wy, wz, emit, 0, 4, NZ0, (nothing,) * 3)
    for f in range(3):
        diag[f, :, :] = 0.5 * sides[f]
    copies = [
        pltpu.make_async_copy(here, there, sems.at[n])
        for n, (here, there) in enumerate(((c, c_out), (v0, v0_out), (g, g_out), (vb, v1_out)))
    ]
    for copy in copies[:3]:
        copy.start()
    sweep(c, va, v0, vb, 0, 4, 0, NZ0)
    copies[3].start()
    residual(c, vb, v0, invq, r, 0, 4, NZ0)

    def coarse(t, held):
        for x, y in cells_of(2):
            for f in range(3):
                own[f, x, y, span(t), :] = mean8(
                    lambda i, j, dz: r[f, i, j, strided(HALO0 + 2 * t + dz), :], x, y
                )
            own[3, x, y, span(t), :] = mean8(
                lambda i, j, dz: k[i, j, strided(PAD + HALO0 + 2 * t + dz), :], x, y
            )
        return held

    over(0, OWN1, coarse)
    for copy in copies:
        copy.wait()


def up_kernel(
    c_in, v0_in, v1_in, g_in, own, below, above, diag,
    p, sums,
    k1, wx1, wy1, wz1, c1, f1, q1, r1, va1, vb1,
    k2, wx2, wy2, wz2, c2, f2, q2, r2, va2, vb2,
    k3, wx3, wy3, wz3, c3, f3, va3, vb3,
    wide1, wide2, wide3, va0, vb0, c0, v00, g, mixed, sems,
):
    lane = lanes_of()
    copies = [
        pltpu.make_async_copy(there, here, sems.at[n])
        for n, (here, there) in enumerate(((va0, v1_in), (c0, c_in), (v00, v0_in), (g, g_in)))
    ]
    for copy in copies:
        copy.start()

    for ref, base, count in ((below, 0, HALO1), (own, HALO1, OWN1), (above, HALO1 + OWN1, HALO1)):

        def fill(t, held):
            for x, y in cells_of(2):
                for f in range(3):
                    f1[f, x, y, span(base + t), :] = ref[f, x, y, span(t), :]
                k1[x, y, span(PAD + base + t), :] = ref[3, x, y, span(t), :]
            return held

        over(0, count, fill)

    def prepare(level, side, nz, k, wx, wy, wz, c, first, invq, va, vb):
        zero_pads(k, cells_of(side), nz)
        zero_pads(va, fields_of(side), nz)
        zero_pads(vb, fields_of(side), nz)
        scale = 4.0**level

        def emit(t, held, x, y, outer, weights, full, total):
            rows = span(t)
            q = RELAX * pl.reciprocal(total)
            for n in range(6):
                c[n, x, y, rows, :] = q * weights[n]
            if invq is not None:
                invq[x, y, rows, :] = (1.0 / (RELAX * scale)) * total
            for f in range(3):
                start = (q * scale) * first[f, x, y, rows, :]
                first[f, x, y, rows, :] = start
                va[f, x, y, span(PAD + t), :] = start
            return held

        coefficients(k, wx, wy, wz, emit, level, side, nz)

    def restrict(mean, side, nz, r, k, first, knext):
        def step(t, held):
            for x, y in cells_of(side):
                for f in range(3):
                    first[f, x, y, span(t), :] = mean(
                        lambda i, j, dz: r[f, i, j, strided(2 * t + dz), :], x, y
                    )
                knext[x, y, span(PAD + t), :] = mean(
                    lambda i, j, dz: k[i, j, strided(PAD + 2 * t + dz), :], x, y
                )
            return held

        over(0, nz, step)

    def widen(e, wide, side, first_row, count):
        def step(t, held):
            for f, x, y in fields_of(side):
                part = e[f, x, y, span(PAD + first_row + t), :]
                wide[f, x, y, strided(2 * t), :] = part
                wide[f, x, y, strided(2 * t + 1), :] = part
            return held

        over(0, count, step)

    def add_coarse(v, wide, side, ratio, lo, hi, first_row):
        def step(t, held):
            for f, x, y in fields_of(side):
                rows = span(PAD + t)
                v[f, x, y, rows, :] = (
                    v[f, x, y, rows, :] + wide[f, x // ratio, y // ratio, span(t - first_row), :]
                )
            return held

        over(lo, hi, step)

    prepare(1, 2, NZ1, k1, wx1, wy1, wz1, c1, f1, q1, va1, vb1)
    sweep(c1, va1, f1, vb1, 1, 2, 0, NZ1)
    residual(c1, vb1, f1, q1, r1, 1, 2, NZ1)
    restrict(mean8, 1, NZ2, r1, k1, f2, k2)

    prepare(2, 1, NZ2, k2, wx2, wy2, wz2, c2, f2, q2, va2, vb2)
    sweep(c2, va2, f2, vb2, 2, 1, 0, NZ2)
    for f in range(3):
        r2[f, 0, 0, span(NZ2), :] = jnp.zeros((8, LANES), jnp.float32)
    residual(c2, vb2, f2, q2, r2, 2, 1, NZ2)
    restrict(lambda read, x, y: mean8_lanes(read), 1, NZ3, r2, k2, f3, k3)

    prepare(3, 1, NZ3, k3, wx3, wy3, wz3, c3, f3, None, va3, vb3)
    sweep(c3, va3, f3, vb3, 3, 1, 0, NZ3)
    sweep(c3, vb3, f3, va3, 3, 1, 0, NZ3)
    sweep(c3, va3, f3, vb3, 3, 1, 0, NZ3)
    sweep(c3, vb3, f3, va3, 3, 1, 0, NZ3)
    sweep(c3, va3, f3, vb3, 3, 1, 0, NZ3)

    widen(vb3, wide3, 1, 0, NZ3)
    add_coarse(vb2, wide3, 1, 1, 0, NZ2, 0)
    sweep(c2, vb2, f2, va2, 2, 1, 0, NZ2)
    sweep(c2, va2, f2, vb2, 2, 1, 0, NZ2)

    lo1, hi1 = HALO1 - 8, HALO1 + OWN1 + 8
    widen(vb2, wide2, 1, lo1 // 2, (hi1 - lo1) // 2)
    add_coarse(vb1, wide2, 2, 2, lo1, hi1, lo1)
    sweep(c1, vb1, f1, va1, 1, 2, lo1, hi1)
    sweep(c1, va1, f1, vb1, 1, 2, lo1, hi1)

    widen(vb1, wide1, 2, HALO1 - HALO0 // 2, 72)
    zero_pads(vb0, fields_of(4), NZ0)
    for copy in copies:
        copy.wait()
    add_coarse(va0, wide1, 4, 2, 0, NZ0, 0)
    sweep(c0, va0, v00, vb0, 0, 4, 0, NZ0)

    def last(t, held):
        held = list(held)
        rows = span(HALO0 + t)
        for x, y in cells_of(4):
            centres, near = neighbours(c0, vb0, 4, 0, x, y, HALO0 + t)
            done = [
                near[f] + (v00[f, x, y, rows, :] + (1.0 - RELAX) * centres[f]) for f in range(3)
            ]
            for f in range(3):
                va0[f, x, y, span(t), :] = done[f]
            for i in range(3):
                gi = g[i, x, y, rows, :]
                for j in range(3):
                    held[3 * i + j] = held[3 * i + j] + gi * done[j]
        return tuple(held)

    nothing = jnp.zeros((8, LANES), jnp.float32)
    fluxes = over(0, OWN0, last, (nothing,) * 9)

    flat = jnp.zeros((1, LANES), jnp.float32)
    one_row = lax.broadcasted_iota(jnp.int32, (1, LANES), 1)
    for i in range(3):
        for j in range(3):
            part = fluxes[3 * i + j]
            if i == j:
                part = part + diag[i, :, :]
            whole = jnp.sum(jnp.sum(part, axis=0, keepdims=True), axis=1, keepdims=True)
            flat = jnp.where(one_row == 3 * i + j, whole, flat)
    sums[...] = flat

    start = lax.axis_index("row") * 32 + lax.axis_index("col") * 4
    for f in range(3):

        def gather(t, held):
            block = nothing
            for x, y in cells_of(4):
                amount = (32 * x + 4 * y + LANES - start) & (LANES - 1)
                piece = pltpu.roll(va0[f, x, y, span(t), :], amount, 1)
                block = jnp.where((lane & 0b1101100) == 32 * x + 4 * y, piece, block)
            mixed[span(t), :] = block
            return held

        over(0, OWN0, gather)
        block = mixed[...].T
        for x in range(8):
            for ylo in range(4):
                begin = (x % 4) * 32 + (x // 4) * 16 + ylo * 4
                p[f, x, pl.ds(ylo, 4, stride=4), :] = block[begin : begin + 4]


def f32(*shape):
    return jax.ShapeDtypeStruct(shape, jnp.float32)


def scratch(*shape):
    return pltpu.VMEM(shape, jnp.float32)


def level_scratch(side, nz, last=False):
    rows = nz + 2 * PAD
    got = [scratch(side, side, rows, LANES)] * 4
    got += [scratch(6, side, side, nz, LANES), scratch(3, side, side, nz, LANES)]
    if not last:
        got += [scratch(side, side, nz, LANES), scratch(3, side, side, nz + 8, LANES)]
    return got + [scratch(3, side, side, rows, LANES)] * 2


def params():
    return pltpu.CompilerParams(vmem_limit_bytes=VMEM_LIMIT)


VM = pl.BlockSpec(memory_space=pltpu.VMEM)
SM = pl.BlockSpec(memory_space=pltpu.SMEM)
HB = pl.BlockSpec(memory_space=pl.ANY)
ROWS0 = NZ0 + 2 * PAD


def conductivities(labels, table):
    return pl.pallas_call(
        look_up,
        out_shape=[f32(LANES, LANES), f32(HALO0, LANES), f32(HALO0, LANES)],
        in_specs=[VM, SM],
        out_specs=[VM] * 3,
        scratch_shapes=[scratch(LANES, LANES)],
        name="look_up",
    )(labels, table)


def down(blocks):
    return pl.pallas_call(
        down_kernel,
        out_shape=[
            f32(6, 4, 4, NZ0, LANES), f32(3, 4, 4, NZ0, LANES), f32(3, 4, 4, ROWS0, LANES),
            f32(3, 4, 4, NZ0, LANES), f32(4, 2, 2, OWN1, LANES), f32(3, 8, LANES),
        ],
        in_specs=[VM],
        out_specs=[HB] * 4 + [VM] * 2,
        scratch_shapes=[scratch(4, 4, ROWS0, LANES)] * 4
        + [
            scratch(6, 4, 4, NZ0, LANES), scratch(3, 4, 4, NZ0, LANES), scratch(3, 4, 4, NZ0, LANES),
            scratch(4, 4, NZ0, LANES), scratch(3, 4, 4, NZ0, LANES),
            scratch(3, 4, 4, ROWS0, LANES), scratch(3, 4, 4, ROWS0, LANES),
            pltpu.SemaphoreType.DMA((4,)),
        ],
        compiler_params=params(),
        name="down",
    )(blocks)


def up(c0, v00, v01, g, own, below, above, diag):
    return pl.pallas_call(
        up_kernel,
        out_shape=[f32(3, 8, 16, LANES), f32(1, LANES)],
        in_specs=[HB] * 4 + [VM] * 4,
        out_specs=[VM] * 2,
        scratch_shapes=level_scratch(2, NZ1) + level_scratch(1, NZ2) + level_scratch(1, NZ3, True)
        + [
            scratch(3, 2, 2, 144, LANES), scratch(3, 1, 1, 80, LANES), scratch(3, 1, 1, 80, LANES),
            scratch(3, 4, 4, ROWS0, LANES), scratch(3, 4, 4, ROWS0, LANES),
            scratch(6, 4, 4, NZ0, LANES), scratch(3, 4, 4, NZ0, LANES), scratch(3, 4, 4, NZ0, LANES),
            scratch(LANES, LANES), pltpu.SemaphoreType.DMA((4,)),
        ],
        compiler_params=params(),
        name="up",
    )(c0, v00, v01, g, own, below, above, diag)


def from_below(x):
    n = lax.axis_size("dep")
    return lax.ppermute(x, "dep", [(i, i + 1) for i in range(n - 1)])


def from_above(x):
    n = lax.axis_size("dep")
    return lax.ppermute(x, "dep", [(i + 1, i) for i in range(n - 1)])


def body(labels, conductivity):
    k, high, low = conductivities(labels, conductivity)
    column = jnp.concatenate([from_below(high), k, from_above(low)], axis=0)
    plane = lax.axis_size("row") * lax.axis_size("col")
    blocks = lax.all_to_all(
        jnp.broadcast_to(column[None], (plane,) + column.shape), ("row", "col"), 0, 0
    )
    c0, v00, v01, g, own, diag = down(blocks)
    below = from_below(own[:, :, :, OWN1 - HALO1 :])
    above = from_above(own[:, :, :, :HALO1])
    p, sums = up(c0, v00, v01, g, own, below, above, diag)
    depth = lax.axis_size("dep")
    parts = lax.all_to_all(jnp.broadcast_to(sums[None], (depth, 1, LANES)), "dep", 0, 0)
    cells = plane * labels.size * depth
    tensor = jnp.sum(parts, axis=(0, 1))[:9].reshape(3, 3) / cells
    return p, tensor


def solution(mesh):
    in_specs = (P("row", "col", "dep"), P())
    out_specs = (P(None, "row", "col", "dep"), P())
    return jax.shard_map(body, mesh=mesh, in_specs=in_specs, out_specs=out_specs, check_vma=False)
```

time: 674 us -> 118 us (0.18)
  starting transfers between devices: 394 us -> 15.6 us
  waiting for transfers between devices: 100 us -> 5 us
  blocking collectives: 124 us -> 52.8 us
  Pallas kernels: 0 us -> 39.6 us
  local copies, waits for them, and re-layouts: 27.5 us -> 3.25 us
  other arithmetic: 21.6 us -> 0.88 us
    ppermute x132 -> x4, starting transfers between devices: 394 us -> 15.6 us  [the longest x2 8.58 us: from_below(): return lax.ppermute(x, 'dep', [(i, i + 1) for i in range(n - 1)])]
    psum x1 -> x0, blocking collectives: 124 us -> none  [body(): summed = lax.psum(partial_sums, ('row', 'col', 'dep'))]
    ppermute x132 -> x4, waiting for transfers between devices: 100 us -> 5 us  [the longest x2 3.81 us: from_above(): return lax.ppermute(x, 'dep', [(i + 1, i) for i in range(n - 1)])]
    all_to_all x0 -> x2, blocking collectives: none -> 52.8 us  [the longest x1 30.2 us: body(): lax.all_to_all(jnp.broadcast_to(sums[None], (depth, 1, LANES)), 'dep', 0, 0)]
    pallas_call x0 -> x3, Pallas kernels: none -> 39.6 us  [the longest x1 21.1 us: up(): pl.pallas_call(up_kernel, out_shape=[f32(3, 8, 16, LANES), f32(1, LANES)]...]
    reshape x7 -> x0, local copies, waits for them, and re-layouts: 22.1 us -> none  [the longest x3 21.1 us: coarsen(): field.reshape(leading + (size_x // 2, 2, size_y // 2, 2, size_z // 2, 2))]
    add x21 -> x0, other arithmetic: 9.45 us -> none  [the longest x1 5.76 us: body(): cell_conduct + jnp.where(labels == phase, conductivity[phase], 0.0)]
    reduce_sum x10 -> x1, other arithmetic: 9.35 us -> 0.02 us  [body(): tensor = jnp.sum(parts, axis=(0, 1))[:9].reshape(3, 3) / cells]
  transfers between devices with their start and end apart: 132 -> 4, of which waited for: 57 -> 3; matrix products, arithmetic and copies ran while one was open for 2% -> 0% of each run, Pallas kernels for 0% -> 0%
where the time goes in v2:
time: 118 us
  blocking collectives  52.8 us (45%)
  Pallas kernels  39.6 us (34%)
  starting transfers between devices  15.6 us (13%)
  waiting for transfers between devices  5 us (4%)
  local copies, waits for them, and re-layouts  3.25 us (3%)
    all_to_all x1, blocking collectives, body(): lax.all_to_all(jnp.broadcast_to(sums[None], (depth, 1, LANES)), 'dep', 0, 0)  30.2 us
    all_to_all x1, blocking collectives, body(): lax.all_to_all(jnp.broadcast_to(column[None], (plane,) + column.shape), (...  22.6 us
    pallas_call x1, Pallas kernels, up(): pl.pallas_call(up_kernel, out_shape=[f32(3, 8, 16, LANES), f32(1, LANES)]...  21.1 us
    pallas_call x1, Pallas kernels, down(): pl.pallas_call(down_kernel, out_shape=[f32(6, 4, 4, NZ0, LANES), f32(3, 4...  16.8 us
    ppermute x2, starting transfers between devices, from_below(): return lax.ppermute(x, 'dep', [(i, i + 1) for i in range(n - 1)])  8.58 us
    ppermute x2, starting transfers between devices, from_above(): return lax.ppermute(x, 'dep', [(i + 1, i) for i in range(n - 1)])  7.06 us
    ppermute x2, waiting for transfers between devices, from_above(): return lax.ppermute(x, 'dep', [(i + 1, i) for i in range(n - 1)])  3.81 us
  transfers between devices with their start and end apart: 4, of which 3 were waited for; matrix products, arithmetic and copies ran while one was open for 0% of the time, Pallas kernels for 0%

profile of v2, /device:TPU:1, one launch (start us, length us, event | category | flops | bytes accessed | tf_op | source)
XLA Modules:
  0.0 117.8 jit_solution(16554357525362284541)
XLA Ops:
  0.6 1.7 %look_up.1 = (f32[128,128]{1,0:T(8,128)}, f32[4,128]{1,0:T(4,128)}, f32[4,128]{1,0:T(4,128)}) custom-call(s32[8,16,128]{2,1,0:T(8,128)} %labels_ref.1, f32[8]{0:T(128)} %table_ref.1), custom_call_target="tpu_custom_call" | custom-call | tf_op jit(solution)/shard_map/look_up/pallas_call | solution.py:493
  2.3 4.9 %collective-permute-start = (f32[4,128]{1,0:T(4,128)}, f32[4,128]{1,0:T(4,128)S(1)}, u32[]{:S(2)}, u32[]{:S(2)}) collective-permute-start(f32[4,128]{1,0:T(4,128)} %get-tuple-element.13), channel_id=1, source_target_pairs={{0,1},{1,2},{2,3},{3,4},{4,5},{5,6},{6,7},{7,8},{8,9},{9,10},{10,1... | collective-permute-start | bytes 6152 | tf_op jit(solution)/shard_map/ppermute | solution.py:544
  7.2 5.1 %collective-permute-start.1 = (f32[4,128]{1,0:T(4,128)}, f32[4,128]{1,0:T(4,128)S(1)}, u32[]{:S(2)}, u32[]{:S(2)}) collective-permute-start(f32[4,128]{1,0:T(4,128)} %get-tuple-element.15), channel_id=1, source_target_pairs={{1,0},{2,1},{3,2},{4,3},{5,4},{6,5},{7,6},{8,7},{9,8},{10,9},{11,1... | collective-permute-start | bytes 6152 | tf_op jit(solution)/shard_map/ppermute | solution.py:549
  12.4 0.0 collective-permute-done
  12.4 1.0 collective-permute-done.1
  13.4 0.8 pad_maximum_fusion
  14.2 0.1 broadcast_in_dim.6
  14.3 22.6 %all_to_all.10.blocks = f32[16,136,128]{2,1,0:T(8,128)} all-to-all(f32[16,136,128]{2,1,0:T(8,128)S(1)} %broadcast_in_dim.6), channel_id=1, replica_groups=mesh['row'=4,'col'=4,'dep'=32] {'row','col'}, dimensions={0} | all-to-all | bytes 2228224 | tf_op jit(solution)/shard_map/all_to_all | solution.py:556
  36.9 16.8 %down.1 = (f32[6,4,4,136,128]{4,3,2,1,0:T(8,128)}, f32[3,4,4,136,128]{4,3,2,1,0:T(8,128)}, f32[3,4,4,152,128]{4,3,2,1,0:T(8,128)}, f32[3,4,4,136,128]{4,3,2,1,0:...) custom-call(f32[16,136,128]{2,1,0:T(8,128)} %all_to_all.10.blocks), custom_call_target="tpu_custom_call" | custom-call | tf_op jit(solution)/shard_map/down/pallas_call | solution.py:504
  53.8 1.1 fusion
  54.9 1.9 %collective-permute-start.3 = (f32[4,2,2,40,128]{4,3,2,1,0:T(8,128)S(1)}, f32[4,2,2,40,128]{4,3,2,1,0:T(8,128)S(1)}, u32[]{:S(2)}, u32[]{:S(2)}) collective-permute-start(f32[4,2,2,40,128]{4,3,2,1,0:T(8,128)S(1)} %get-tuple-element.24), channel_id=1, source_target_pairs={{1,0},{2,1},{3,2},{4,3},{5,4},{6,5},{7,6},{8,7},{9,8},{10,9},{11,1... | collective-permute-start | bytes 983048 | tf_op jit(solution)/shard_map/ppermute | solution.py:549
  56.8 3.7 %collective-permute-start.2 = (f32[4,2,2,40,128]{4,3,2,1,0:T(8,128)S(1)}, f32[4,2,2,40,128]{4,3,2,1,0:T(8,128)S(1)}, u32[]{:S(2)}, u32[]{:S(2)}) collective-permute-start(f32[4,2,2,40,128]{4,3,2,1,0:T(8,128)S(1)} %get-tuple-element.25), channel_id=1, source_target_pairs={{0,1},{1,2},{2,3},{3,4},{4,5},{5,6},{6,7},{7,8},{8,9},{9,10},{10,1... | collective-permute-start | bytes 983048 | tf_op jit(solution)/shard_map/ppermute | solution.py:544
  60.5 2.8 %collective-permute-done.3.above = f32[4,2,2,40,128]{4,3,2,1,0:T(8,128)S(1)} collective-permute-done((f32[4,2,2,40,128]{4,3,2,1,0:T(8,128)S(1)}, f32[4,2,2,40,128]{4,3,2,1,0:T(8,128)S(1)}, u32[]{:S(2)}, u32[]{:S(2)}) %collective-permute-start.3) | collective-permute-done | bytes 327712 | tf_op jit(solution)/shard_map/ppermute | solution.py:549
  63.3 0.0 copy-start
  63.3 1.2 %collective-permute-done.2.below = f32[4,2,2,40,128]{4,3,2,1,0:T(8,128)S(1)} collective-permute-done((f32[4,2,2,40,128]{4,3,2,1,0:T(8,128)S(1)}, f32[4,2,2,40,128]{4,3,2,1,0:T(8,128)S(1)}, u32[]{:S(2)}, u32[]{:S(2)}) %collective-permute-start.2) | collective-permute-done | bytes 327712 | tf_op jit(solution)/shard_map/ppermute | solution.py:544
  64.5 0.0 copy-start.1
  64.5 0.0 copy-done
  64.5 0.7 copy-done.1
  65.2 21.1 %up.1 = (f32[3,8,16,128]{3,2,1,0:T(8,128)}, f32[1,128]{1,0:T(1,128)}) custom-call(f32[6,4,4,136,128]{4,3,2,1,0:T(8,128)} %get-tuple-element.16.c_in, f32[3,4,4,136,128]{4,3,2,1,0:T(8,128)} %get-tuple-element.17.v0_in, f32[3,4,4,152,128]{4,3,2,1,0:T(8,128)} %get-tuple-element.18.v1_in, f32[3,4,4,136,128]{4,3,2,1,0:T(8,128)} %get-tuple-element.19.g_in, ...), custom_call_target="tpu_custom_call" | custom-call | tf_op jit(solution)/shard_map/up/pallas_call | solution.py:525
  86.3 0.7 broadcast_in_dim.16
  86.9 30.2 %all_to_all.11 = f32[32,1,128]{2,1,0:T(1,128)S(1)} all-to-all(f32[32,1,128]{2,1,0:T(1,128)S(1)} %broadcast_in_dim.16), channel_id=1, replica_groups=mesh['row'=4,'col'=4,'dep'=32] {'dep'}, dimensions={0} | all-to-all | bytes 32768 | tf_op jit(solution)/shard_map/all_to_all | solution.py:564
  117.2 0.7 div.6
  (2 shorter events, 0.0 us)
Async XLA Ops:
  2.3 10.1 %collective-permute-start = (f32[4,128]{1,0:T(4,128)}, f32[4,128]{1,0:T(4,128)S(1)}, u32[]{:S(2)}, u32[]{:S(2)}) collective-permute-start(f32[4,128]{1,0:T(4,128)} %get-tuple-element.13), channel_id=1, source_target_pairs={{0,1},{1,2},{2,3},{3,4},{4,5},{5,6},{6,7},{7,8},{8,9},{9,10},{10,1... | collective-permute-start | bytes 6152 | tf_op jit(solution)/shard_map/ppermute | solution.py:544
  7.2 6.2 %collective-permute-start.1 = (f32[4,128]{1,0:T(4,128)}, f32[4,128]{1,0:T(4,128)S(1)}, u32[]{:S(2)}, u32[]{:S(2)}) collective-permute-start(f32[4,128]{1,0:T(4,128)} %get-tuple-element.15), channel_id=1, source_target_pairs={{1,0},{2,1},{3,2},{4,3},{5,4},{6,5},{7,6},{8,7},{9,8},{10,9},{11,1... | collective-permute-start | bytes 6152 | tf_op jit(solution)/shard_map/ppermute | solution.py:549
  54.9 8.4 %collective-permute-start.3 = (f32[4,2,2,40,128]{4,3,2,1,0:T(8,128)S(1)}, f32[4,2,2,40,128]{4,3,2,1,0:T(8,128)S(1)}, u32[]{:S(2)}, u32[]{:S(2)}) collective-permute-start(f32[4,2,2,40,128]{4,3,2,1,0:T(8,128)S(1)} %get-tuple-element.24), channel_id=1, source_target_pairs={{1,0},{2,1},{3,2},{4,3},{5,4},{6,5},{7,6},{8,7},{9,8},{10,9},{11,1... | collective-permute-start | bytes 983048 | tf_op jit(solution)/shard_map/ppermute | solution.py:549
  56.8 7.7 %collective-permute-start.2 = (f32[4,2,2,40,128]{4,3,2,1,0:T(8,128)S(1)}, f32[4,2,2,40,128]{4,3,2,1,0:T(8,128)S(1)}, u32[]{:S(2)}, u32[]{:S(2)}) collective-permute-start(f32[4,2,2,40,128]{4,3,2,1,0:T(8,128)S(1)} %get-tuple-element.25), channel_id=1, source_target_pairs={{0,1},{1,2},{2,3},{3,4},{4,5},{5,6},{6,7},{7,8},{8,9},{9,10},{10,1... | collective-permute-start | bytes 983048 | tf_op jit(solution)/shard_map/ppermute | solution.py:544
  63.3 1.2 %copy-start = (f32[4,2,2,40,128]{4,3,2,1,0:T(8,128)}, f32[4,2,2,40,128]{4,3,2,1,0:T(8,128)S(1)}, u32[]{:S(2)}) copy-start(f32[4,2,2,40,128]{4,3,2,1,0:T(8,128)S(1)} %collective-permute-done.3.above) | copy-start | bytes 983044
  64.5 0.7 copy-start.1

commit v3 on v2

--- a/solution.py
+++ b/solution.py
@@ -1,3 +1,5 @@
+import functools
+
 import jax
 import jax.numpy as jnp
 from jax import lax
@@ -17,7 +19,8 @@
 NZ1 = OWN1 + 2 * HALO1
 NZ2 = NZ1 // 2
 NZ3 = 40
-VMEM_LIMIT = 56 * 1024 * 1024
+GROUPS = {4: 4, 2: 9, 1: 18}
+VMEM_LIMIT = 34 * 1024 * 1024
 
 
 def lanes_of(shape=(8, LANES)):
@@ -40,14 +43,23 @@
     return (2.0 * a) * b * pl.reciprocal(jnp.maximum(a + b, 1e-30))
 
 
-def over(lo, hi, step, carry=0):
-    if hi - lo <= 80:
-        for t in range(lo, hi, 8):
-            carry = step(t, carry)
-        return carry
-    return lax.fori_loop(
-        0, (hi - lo) // 8, lambda i, held: step(pl.multiple_of(lo + 8 * i, 8), held), carry
-    )
+def over(side, lo, hi, step, carry=0):
+    group = GROUPS[side]
+    whole = (hi - lo) // (8 * group)
+    if whole <= 1:
+        whole = 0
+
+    def some(i, held):
+        first = pl.multiple_of(lo + 8 * group * i, 8)
+        for n in range(group):
+            held = step(first + 8 * n, held)
+        return held
+
+    if whole:
+        carry = lax.fori_loop(0, whole, some, carry)
+    for t in range(lo + 8 * group * whole, hi, 8):
+        carry = step(t, carry)
+    return carry
 
 
 def zero_pads(ref, lead, nz):
@@ -113,7 +125,7 @@
             wz[x, y, rows, :] = harmonic(kc, k[x, y, span(PAD + t + 1), :])
         return held
 
-    over(0, nz, faces)
+    over(side, 0, nz, faces)
 
     def cells(t, held):
         rows = span(PAD + t)
@@ -143,7 +155,7 @@
             held = emit(t, held, x, y, outer, weights, full, total)
         return held
 
-    return over(0, nz, cells, carry)
+    return over(side, 0, nz, cells, carry)
 
 
 def neighbours(c, v, side, level, x, y, t):
@@ -168,7 +180,7 @@
                 )
         return held
 
-    over(lo, hi, step)
+    over(side, lo, hi, step)
 
 
 def residual(c, v, first, invq, r, level, side, nz):
@@ -182,7 +194,7 @@
                 ) * scale
         return held
 
-    over(0, nz, step)
+    over(side, 0, nz, step)
 
 
 def mean8(read, x, y):
@@ -218,7 +230,7 @@
 
 
 def down_kernel(
-    blocks, c_out, v0_out, v1_out, g_out, own, diag, k, wx, wy, wz, c, v0, g, invq, r, va, vb, sems
+    blocks, c_out, v0_out, v1_out, g_out, own, low, high, diag, k, wx, wy, wz, c, v0, g, invq, r, va, vb, sems
 ):
     lane = lanes_of()
     zero_pads(k, cells_of(4), NZ0)
@@ -239,7 +251,7 @@
             k[x, y, span(PAD + t), :] = tiles[4 * x + y]
         return held
 
-    over(0, NZ0, place)
+    over(4, 0, NZ0, place)
 
     def emit(t, held, x, y, outer, weights, full, total):
         rows = span(t)
@@ -287,13 +299,17 @@
             )
         return held
 
-    over(0, OWN1, coarse)
+    over(4, 0, OWN1, coarse)
+    for n in range(4):
+        for x, y in cells_of(2):
+            low[n, x, y, :, :] = own[n, x, y, pl.ds(0, HALO1), :]
+            high[n, x, y, :, :] = own[n, x, y, pl.ds(OWN1 - HALO1, HALO1), :]
     for copy in copies:
         copy.wait()
 
 
 def up_kernel(
-    c_in, v0_in, v1_in, g_in, own, below, above, diag,
+    share, c_in, v0_in, v1_in, g_in, own, below, above, diag,
     p, sums,
     k1, wx1, wy1, wz1, c1, f1, q1, r1, va1, vb1,
     k2, wx2, wy2, wz2, c2, f2, q2, r2, va2, vb2,
@@ -317,7 +333,7 @@
                 k1[x, y, span(PAD + base + t), :] = ref[3, x, y, span(t), :]
             return held
 
-        over(0, count, fill)
+        over(2, 0, count, fill)
 
     def prepare(level, side, nz, k, wx, wy, wz, c, first, invq, va, vb):
         zero_pads(k, cells_of(side), nz)
@@ -352,7 +368,7 @@
                 )
             return held
 
-        over(0, nz, step)
+        over(2 * side, 0, nz, step)
 
     def widen(e, wide, side, first_row, count):
         def step(t, held):
@@ -362,7 +378,7 @@
                 wide[f, x, y, strided(2 * t + 1), :] = part
             return held
 
-        over(0, count, step)
+        over(2 * side, 0, count, step)
 
     def add_coarse(v, wide, side, ratio, lo, hi, first_row):
         def step(t, held):
@@ -373,7 +389,7 @@
                 )
             return held
 
-        over(lo, hi, step)
+        over(side, lo, hi, step)
 
     prepare(1, 2, NZ1, k1, wx1, wy1, wz1, c1, f1, q1, va1, vb1)
     sweep(c1, va1, f1, vb1, 1, 2, 0, NZ1)
@@ -429,7 +445,7 @@
         return tuple(held)
 
     nothing = jnp.zeros((8, LANES), jnp.float32)
-    fluxes = over(0, OWN0, last, (nothing,) * 9)
+    fluxes = over(4, 0, OWN0, last, (nothing,) * 9)
 
     flat = jnp.zeros((1, LANES), jnp.float32)
     one_row = lax.broadcasted_iota(jnp.int32, (1, LANES), 1)
@@ -440,7 +456,9 @@
                 part = part + diag[i, :, :]
             whole = jnp.sum(jnp.sum(part, axis=0, keepdims=True), axis=1, keepdims=True)
             flat = jnp.where(one_row == 3 * i + j, whole, flat)
-    sums[...] = flat
+    flat = flat * share
+    for n in range(sums.shape[0]):
+        sums[n, :, :] = flat
 
     start = lax.axis_index("row") * 32 + lax.axis_index("col") * 4
     for f in range(3):
@@ -454,7 +472,7 @@
             mixed[span(t), :] = block
             return held
 
-        over(0, OWN0, gather)
+        over(4, 0, OWN0, gather)
         block = mixed[...].T
         for x in range(8):
             for ylo in range(4):
@@ -505,10 +523,11 @@
         down_kernel,
         out_shape=[
             f32(6, 4, 4, NZ0, LANES), f32(3, 4, 4, NZ0, LANES), f32(3, 4, 4, ROWS0, LANES),
-            f32(3, 4, 4, NZ0, LANES), f32(4, 2, 2, OWN1, LANES), f32(3, 8, LANES),
+            f32(3, 4, 4, NZ0, LANES), f32(4, 2, 2, OWN1, LANES), f32(4, 2, 2, HALO1, LANES),
+            f32(4, 2, 2, HALO1, LANES), f32(3, 8, LANES),
         ],
         in_specs=[VM],
-        out_specs=[HB] * 4 + [VM] * 2,
+        out_specs=[HB] * 4 + [VM] * 4,
         scratch_shapes=[scratch(4, 4, ROWS0, LANES)] * 4
         + [
             scratch(6, 4, 4, NZ0, LANES), scratch(3, 4, 4, NZ0, LANES), scratch(3, 4, 4, NZ0, LANES),
@@ -521,10 +540,10 @@
     )(blocks)
 
 
-def up(c0, v00, v01, g, own, below, above, diag):
+def up(c0, v00, v01, g, own, below, above, diag, depth, cells):
     return pl.pallas_call(
-        up_kernel,
-        out_shape=[f32(3, 8, 16, LANES), f32(1, LANES)],
+        functools.partial(up_kernel, 1.0 / cells),
+        out_shape=[f32(3, 8, 16, LANES), f32(depth, 1, LANES)],
         in_specs=[HB] * 4 + [VM] * 4,
         out_specs=[VM] * 2,
         scratch_shapes=level_scratch(2, NZ1) + level_scratch(1, NZ2) + level_scratch(1, NZ3, True)
@@ -556,14 +575,14 @@
     blocks = lax.all_to_all(
         jnp.broadcast_to(column[None], (plane,) + column.shape), ("row", "col"), 0, 0
     )
-    c0, v00, v01, g, own, diag = down(blocks)
-    below = from_below(own[:, :, :, OWN1 - HALO1 :])
-    above = from_above(own[:, :, :, :HALO1])
-    p, sums = up(c0, v00, v01, g, own, below, above, diag)
+    c0, v00, v01, g, own, low, high, diag = down(blocks)
+    above = from_above(low)
+    below = from_below(high)
     depth = lax.axis_size("dep")
-    parts = lax.all_to_all(jnp.broadcast_to(sums[None], (depth, 1, LANES)), "dep", 0, 0)
     cells = plane * labels.size * depth
-    tensor = jnp.sum(parts, axis=(0, 1))[:9].reshape(3, 3) / cells
+    p, sums = up(c0, v00, v01, g, own, below, above, diag, depth, cells)
+    parts = lax.all_to_all(sums, "dep", 0, 0)
+    tensor = jnp.sum(parts, axis=(0, 1))[:9].reshape(3, 3)
     return p, tensor
 
 

time: 118 us -> 102 us (0.86)
  Pallas kernels: 39.6 us -> 26.1 us
  blocking collectives: 52.8 us -> 50.1 us
  local copies, waits for them, and re-layouts: 3.25 us -> 0.74 us
  waiting for transfers between devices: 5 us -> 7.47 us
    pallas_call x1, Pallas kernels: 21.1 us -> 13.7 us  [up(): pl.pallas_call(functools.partial(up_kernel, 1.0 / cells), out_shape=[f32(...]
    pallas_call x1, Pallas kernels: 16.8 us -> 10.7 us  [down(): pl.pallas_call(down_kernel, out_shape=[f32(6, 4, 4, NZ0, LANES), f32(3, 4...]
    all_to_all x1, blocking collectives: 30.2 us -> 27.6 us  [body(): parts = lax.all_to_all(sums, 'dep', 0, 0)]
    ppermute x2, waiting for transfers between devices: 3.81 us -> 5.39 us  [from_above(): return lax.ppermute(x, 'dep', [(i + 1, i) for i in range(n - 1)])]
where the time goes in v3:
time: 102 us
  blocking collectives  50.1 us (49%)
  Pallas kernels  26.1 us (26%)
  starting transfers between devices  15.6 us (15%)
  waiting for transfers between devices  7.47 us (7%)
    all_to_all x1, blocking collectives, body(): parts = lax.all_to_all(sums, 'dep', 0, 0)  27.6 us
    all_to_all x1, blocking collectives, body(): lax.all_to_all(jnp.broadcast_to(column[None], (plane,) + column.shape), (...  22.5 us
    pallas_call x1, Pallas kernels, up(): pl.pallas_call(functools.partial(up_kernel, 1.0 / cells), out_shape=[f32(...  13.7 us
    pallas_call x1, Pallas kernels, down(): pl.pallas_call(down_kernel, out_shape=[f32(6, 4, 4, NZ0, LANES), f32(3, 4...  10.7 us
    ppermute x2, starting transfers between devices, from_below(): return lax.ppermute(x, 'dep', [(i, i + 1) for i in range(n - 1)])  8.58 us
    ppermute x2, starting transfers between devices, from_above(): return lax.ppermute(x, 'dep', [(i + 1, i) for i in range(n - 1)])  7.06 us
    ppermute x2, waiting for transfers between devices, from_above(): return lax.ppermute(x, 'dep', [(i + 1, i) for i in range(n - 1)])  5.39 us
    ppermute x2, waiting for transfers between devices, from_below(): return lax.ppermute(x, 'dep', [(i, i + 1) for i in range(n - 1)])  2.07 us
  transfers between devices with their start and end apart: 4, of which 3 were waited for; matrix products, arithmetic and copies ran while one was open for 0% of the time, Pallas kernels for 0%

profile of v3, /device:TPU:1, one launch (start us, length us, event | category | flops | bytes accessed | tf_op | source)
XLA Modules:
  0.0 101.6 jit_solution(14593758926744031814)
XLA Ops:
  0.6 1.7 %look_up.1 = (f32[128,128]{1,0:T(8,128)}, f32[4,128]{1,0:T(4,128)}, f32[4,128]{1,0:T(4,128)}) custom-call(s32[8,16,128]{2,1,0:T(8,128)} %labels_ref.1, f32[8]{0:T(128)} %table_ref.1), custom_call_target="tpu_custom_call" | custom-call | tf_op jit(solution)/shard_map/look_up/pallas_call | solution.py:511
  2.3 4.9 %collective-permute-start = (f32[4,128]{1,0:T(4,128)}, f32[4,128]{1,0:T(4,128)S(1)}, u32[]{:S(2)}, u32[]{:S(2)}) collective-permute-start(f32[4,128]{1,0:T(4,128)} %get-tuple-element.15), channel_id=1, source_target_pairs={{0,1},{1,2},{2,3},{3,4},{4,5},{5,6},{6,7},{7,8},{8,9},{9,10},{10,1... | collective-permute-start | bytes 6152 | tf_op jit(solution)/shard_map/ppermute | solution.py:563
  7.2 5.1 %collective-permute-start.1 = (f32[4,128]{1,0:T(4,128)}, f32[4,128]{1,0:T(4,128)S(1)}, u32[]{:S(2)}, u32[]{:S(2)}) collective-permute-start(f32[4,128]{1,0:T(4,128)} %get-tuple-element.17), channel_id=1, source_target_pairs={{1,0},{2,1},{3,2},{4,3},{5,4},{6,5},{7,6},{8,7},{9,8},{10,9},{11,1... | collective-permute-start | bytes 6152 | tf_op jit(solution)/shard_map/ppermute | solution.py:568
  12.4 0.0 collective-permute-done
  12.4 1.0 collective-permute-done.1
  13.4 0.8 pad_maximum_fusion
  14.2 0.1 broadcast_in_dim.2
  14.3 22.5 %all_to_all.10.blocks = f32[16,136,128]{2,1,0:T(8,128)S(1)} all-to-all(f32[16,136,128]{2,1,0:T(8,128)S(1)} %broadcast_in_dim.2), channel_id=1, replica_groups=mesh['row'=4,'col'=4,'dep'=32] {'row','col'}, dimensions={0} | all-to-all | bytes 2228224 | tf_op jit(solution)/shard_map/all_to_all | solution.py:575
  36.8 10.7 %down.1 = (f32[6,4,4,136,128]{4,3,2,1,0:T(8,128)S(1)}, f32[3,4,4,136,128]{4,3,2,1,0:T(8,128)S(1)}, f32[3,4,4,152,128]{4,3,2,1,0:T(8,128)S(1)}, f32[3,4,4,136,128...) custom-call(f32[16,136,128]{2,1,0:T(8,128)S(1)} %all_to_all.10.blocks), custom_call_target="tpu_custom_call" | custom-call | tf_op jit(solution)/shard_map/down/pallas_call | solution.py:522
  47.5 3.7 %collective-permute-start.2 = (f32[4,2,2,40,128]{4,3,2,1,0:T(8,128)S(1)}, f32[4,2,2,40,128]{4,3,2,1,0:T(8,128)S(1)}, u32[]{:S(2)}, u32[]{:S(2)}) collective-permute-start(f32[4,2,2,40,128]{4,3,2,1,0:T(8,128)S(1)} %get-tuple-element.23), channel_id=1, source_target_pairs={{0,1},{1,2},{2,3},{3,4},{4,5},{5,6},{6,7},{7,8},{8,9},{9,10},{10,1... | collective-permute-start | bytes 983048 | tf_op jit(solution)/shard_map/ppermute | solution.py:563
  51.2 1.9 %collective-permute-start.3 = (f32[4,2,2,40,128]{4,3,2,1,0:T(8,128)S(1)}, f32[4,2,2,40,128]{4,3,2,1,0:T(8,128)S(1)}, u32[]{:S(2)}, u32[]{:S(2)}) collective-permute-start(f32[4,2,2,40,128]{4,3,2,1,0:T(8,128)S(1)} %get-tuple-element.24), channel_id=1, source_target_pairs={{1,0},{2,1},{3,2},{4,3},{5,4},{6,5},{7,6},{8,7},{9,8},{10,9},{11,1... | collective-permute-start | bytes 983048 | tf_op jit(solution)/shard_map/ppermute | solution.py:568
  53.1 2.1 %collective-permute-done.2.below = f32[4,2,2,40,128]{4,3,2,1,0:T(8,128)S(1)} collective-permute-done((f32[4,2,2,40,128]{4,3,2,1,0:T(8,128)S(1)}, f32[4,2,2,40,128]{4,3,2,1,0:T(8,128)S(1)}, u32[]{:S(2)}, u32[]{:S(2)}) %collective-permute-start.2) | collective-permute-done | bytes 327712 | tf_op jit(solution)/shard_map/ppermute | solution.py:563
  55.2 4.4 %collective-permute-done.3.above = f32[4,2,2,40,128]{4,3,2,1,0:T(8,128)S(1)} collective-permute-done((f32[4,2,2,40,128]{4,3,2,1,0:T(8,128)S(1)}, f32[4,2,2,40,128]{4,3,2,1,0:T(8,128)S(1)}, u32[]{:S(2)}, u32[]{:S(2)}) %collective-permute-start.3) | collective-permute-done | bytes 327712 | tf_op jit(solution)/shard_map/ppermute | solution.py:568
  59.6 13.7 %up.1 = (f32[3,8,16,128]{3,2,1,0:T(8,128)}, f32[32,1,128]{2,1,0:T(1,128)S(1)}) custom-call(f32[6,4,4,136,128]{4,3,2,1,0:T(8,128)S(1)} %get-tuple-element.18.c_in, f32[3,4,4,136,128]{4,3,2,1,0:T(8,128)S(1)} %get-tuple-element.19.v0_in, f32[3,4,4,152,128]{4,3,2,1,0:T(8,128)S(1)} %get-tuple-element.20.v1_in, f32[3,4,4,136,128]{4,3,2,1,0:T(8,128)S(1)} %get-tuple-element.21.g_in, ...), custom_call_target="tpu_custom_call" | custom-call | tf_op jit(solution)/shard_map/up/pallas_call | solution.py:544
  73.3 27.6 %all_to_all.11 = f32[32,1,128]{2,1,0:T(1,128)S(1)} all-to-all(f32[32,1,128]{2,1,0:T(1,128)S(1)} %get-tuple-element.27), channel_id=1, replica_groups=mesh['row'=4,'col'=4,'dep'=32] {'dep'}, dimensions={0} | all-to-all | bytes 32768 | tf_op jit(solution)/shard_map/all_to_all | solution.py:584
  100.9 0.1 reduce_sum.9
  101.0 0.7 reshape.8
Async XLA Ops:
  2.3 10.1 %collective-permute-start = (f32[4,128]{1,0:T(4,128)}, f32[4,128]{1,0:T(4,128)S(1)}, u32[]{:S(2)}, u32[]{:S(2)}) collective-permute-start(f32[4,128]{1,0:T(4,128)} %get-tuple-element.15), channel_id=1, source_target_pairs={{0,1},{1,2},{2,3},{3,4},{4,5},{5,6},{6,7},{7,8},{8,9},{9,10},{10,1... | collective-permute-start | bytes 6152 | tf_op jit(solution)/shard_map/ppermute | solution.py:563
  7.2 6.2 %collective-permute-start.1 = (f32[4,128]{1,0:T(4,128)}, f32[4,128]{1,0:T(4,128)S(1)}, u32[]{:S(2)}, u32[]{:S(2)}) collective-permute-start(f32[4,128]{1,0:T(4,128)} %get-tuple-element.17), channel_id=1, source_target_pairs={{1,0},{2,1},{3,2},{4,3},{5,4},{6,5},{7,6},{8,7},{9,8},{10,9},{11,1... | collective-permute-start | bytes 6152 | tf_op jit(solution)/shard_map/ppermute | solution.py:568
  47.5 7.7 %collective-permute-start.2 = (f32[4,2,2,40,128]{4,3,2,1,0:T(8,128)S(1)}, f32[4,2,2,40,128]{4,3,2,1,0:T(8,128)S(1)}, u32[]{:S(2)}, u32[]{:S(2)}) collective-permute-start(f32[4,2,2,40,128]{4,3,2,1,0:T(8,128)S(1)} %get-tuple-element.23), channel_id=1, source_target_pairs={{0,1},{1,2},{2,3},{3,4},{4,5},{5,6},{6,7},{7,8},{8,9},{9,10},{10,1... | collective-permute-start | bytes 983048 | tf_op jit(solution)/shard_map/ppermute | solution.py:563
  51.2 8.4 %collective-permute-start.3 = (f32[4,2,2,40,128]{4,3,2,1,0:T(8,128)S(1)}, f32[4,2,2,40,128]{4,3,2,1,0:T(8,128)S(1)}, u32[]{:S(2)}, u32[]{:S(2)}) collective-permute-start(f32[4,2,2,40,128]{4,3,2,1,0:T(8,128)S(1)} %get-tuple-element.24), channel_id=1, source_target_pairs={{1,0},{2,1},{3,2},{4,3},{5,4},{6,5},{7,6},{8,7},{9,8},{10,9},{11,1... | collective-permute-start | bytes 983048 | tf_op jit(solution)/shard_map/ppermute | solution.py:568

commit v4 on v3

--- a/solution.py
+++ b/solution.py
@@ -144,8 +144,8 @@
                 edges.x_first if x == 0 else None,
                 edges.y_last if y == last else None,
                 edges.y_first if y == 0 else None,
-                k[x, y, span(PAD + t + 1), :] == 0.0,
-                k[x, y, span(PAD + t - 1), :] == 0.0,
+                weights[4] == 0.0,
+                weights[5] == 0.0,
             ]
             full = [w if o is None else jnp.where(o, kc, w) for o, w in zip(outer, weights)]
             total = full[0]
@@ -170,27 +170,29 @@
     return centres, sums
 
 
-def sweep(c, v, first, out, level, side, lo, hi):
+def sweep(c, v, first, out, level, side, lo, hi, base=0):
     def step(t, held):
         for x, y in cells_of(side):
             centres, sums = neighbours(c, v, side, level, x, y, t)
             for f in range(3):
                 out[f, x, y, span(PAD + t), :] = sums[f] + (
-                    first[f, x, y, span(t), :] + (1.0 - RELAX) * centres[f]
+                    (2.0 - RELAX) * centres[f]
+                    if first is v
+                    else first[f, x, y, span(base + t), :] + (1.0 - RELAX) * centres[f]
                 )
         return held
 
     over(side, lo, hi, step)
 
 
-def residual(c, v, first, invq, r, level, side, nz):
+def residual(c, v, first, invq, r, level, side, nz, base=0):
     def step(t, held):
         for x, y in cells_of(side):
             centres, sums = neighbours(c, v, side, level, x, y, t)
             scale = invq[x, y, span(t), :]
             for f in range(3):
                 r[f, x, y, span(t), :] = (
-                    sums[f] + (first[f, x, y, span(t), :] - RELAX * centres[f])
+                    sums[f] + (first[f, x, y, span(base + t), :] - RELAX * centres[f])
                 ) * scale
         return held
 
@@ -230,14 +232,14 @@
 
 
 def down_kernel(
-    blocks, c_out, v0_out, v1_out, g_out, own, low, high, diag, k, wx, wy, wz, c, v0, g, invq, r, va, vb, sems
+    blocks, c_out, v0_out, v1_out, g_out, own, low, high, diag, k, wx, wy, wz, c, g, invq, r, va, vb, sems
 ):
     lane = lanes_of()
     zero_pads(k, cells_of(4), NZ0)
     zero_pads(va, fields_of(4), NZ0)
     zero_pads(vb, fields_of(4), NZ0)
 
-    def place(t, held):
+    for t in range(0, NZ0, 8):
         tiles = [blocks[n, span(t), :] for n in range(16)]
         for bit, stride in ((0, 4), (1, 8), (2, 32), (3, 64)):
             dist = 1 << bit
@@ -249,9 +251,6 @@
                     tiles[i + dist] = jnp.where(clear, turned(a, -stride), b)
         for x, y in cells_of(4):
             k[x, y, span(PAD + t), :] = tiles[4 * x + y]
-        return held
-
-    over(4, 0, NZ0, place)
 
     def emit(t, held, x, y, outer, weights, full, total):
         rows = span(t)
@@ -265,7 +264,6 @@
         for f in range(3):
             up, down = full[2 * f], full[2 * f + 1]
             first = q * (down - up)
-            v0[f, x, y, rows, :] = first
             va[f, x, y, span(PAD + t), :] = first
             upper, lower = outer[2 * f], outer[2 * f + 1]
             half_up = up if upper is None else jnp.where(upper, 0.5 * up, up)
@@ -280,13 +278,13 @@
         diag[f, :, :] = 0.5 * sides[f]
     copies = [
         pltpu.make_async_copy(here, there, sems.at[n])
-        for n, (here, there) in enumerate(((c, c_out), (v0, v0_out), (g, g_out), (vb, v1_out)))
+        for n, (here, there) in enumerate(((c, c_out), (va, v0_out), (g, g_out), (vb, v1_out)))
     ]
     for copy in copies[:3]:
         copy.start()
-    sweep(c, va, v0, vb, 0, 4, 0, NZ0)
+    sweep(c, va, va, vb, 0, 4, 0, NZ0)
     copies[3].start()
-    residual(c, vb, v0, invq, r, 0, 4, NZ0)
+    residual(c, vb, va, invq, r, 0, 4, NZ0, PAD)
 
     def coarse(t, held):
         for x, y in cells_of(2):
@@ -426,7 +424,7 @@
     for copy in copies:
         copy.wait()
     add_coarse(va0, wide1, 4, 2, 0, NZ0, 0)
-    sweep(c0, va0, v00, vb0, 0, 4, 0, NZ0)
+    sweep(c0, va0, v00, vb0, 0, 4, 0, NZ0, PAD)
 
     def last(t, held):
         held = list(held)
@@ -434,7 +432,8 @@
         for x, y in cells_of(4):
             centres, near = neighbours(c0, vb0, 4, 0, x, y, HALO0 + t)
             done = [
-                near[f] + (v00[f, x, y, rows, :] + (1.0 - RELAX) * centres[f]) for f in range(3)
+                near[f] + (v00[f, x, y, span(PAD + HALO0 + t), :] + (1.0 - RELAX) * centres[f])
+                for f in range(3)
             ]
             for f in range(3):
                 va0[f, x, y, span(t), :] = done[f]
@@ -447,32 +446,28 @@
     nothing = jnp.zeros((8, LANES), jnp.float32)
     fluxes = over(4, 0, OWN0, last, (nothing,) * 9)
 
-    flat = jnp.zeros((1, LANES), jnp.float32)
-    one_row = lax.broadcasted_iota(jnp.int32, (1, LANES), 1)
+    tensor = jnp.zeros((3, 3), jnp.float32)
+    place = [lax.broadcasted_iota(jnp.int32, (3, 3), n) for n in range(2)]
     for i in range(3):
         for j in range(3):
             part = fluxes[3 * i + j]
             if i == j:
                 part = part + diag[i, :, :]
             whole = jnp.sum(jnp.sum(part, axis=0, keepdims=True), axis=1, keepdims=True)
-            flat = jnp.where(one_row == 3 * i + j, whole, flat)
-    flat = flat * share
+            tensor = jnp.where((place[0] == i) & (place[1] == j), whole, tensor)
+    tensor = tensor * share
     for n in range(sums.shape[0]):
-        sums[n, :, :] = flat
+        sums[n, :, :] = tensor
 
     start = lax.axis_index("row") * 32 + lax.axis_index("col") * 4
     for f in range(3):
-
-        def gather(t, held):
+        for t in range(0, OWN0, 8):
             block = nothing
             for x, y in cells_of(4):
                 amount = (32 * x + 4 * y + LANES - start) & (LANES - 1)
                 piece = pltpu.roll(va0[f, x, y, span(t), :], amount, 1)
                 block = jnp.where((lane & 0b1101100) == 32 * x + 4 * y, piece, block)
             mixed[span(t), :] = block
-            return held
-
-        over(4, 0, OWN0, gather)
         block = mixed[...].T
         for x in range(8):
             for ylo in range(4):
@@ -522,7 +517,7 @@
     return pl.pallas_call(
         down_kernel,
         out_shape=[
-            f32(6, 4, 4, NZ0, LANES), f32(3, 4, 4, NZ0, LANES), f32(3, 4, 4, ROWS0, LANES),
+            f32(6, 4, 4, NZ0, LANES), f32(3, 4, 4, ROWS0, LANES), f32(3, 4, 4, ROWS0, LANES),
             f32(3, 4, 4, NZ0, LANES), f32(4, 2, 2, OWN1, LANES), f32(4, 2, 2, HALO1, LANES),
             f32(4, 2, 2, HALO1, LANES), f32(3, 8, LANES),
         ],
@@ -530,8 +525,8 @@
         out_specs=[HB] * 4 + [VM] * 4,
         scratch_shapes=[scratch(4, 4, ROWS0, LANES)] * 4
         + [
-            scratch(6, 4, 4, NZ0, LANES), scratch(3, 4, 4, NZ0, LANES), scratch(3, 4, 4, NZ0, LANES),
-            scratch(4, 4, NZ0, LANES), scratch(3, 4, 4, NZ0, LANES),
+            scratch(6, 4, 4, NZ0, LANES), scratch(3, 4, 4, NZ0, LANES), scratch(4, 4, NZ0, LANES),
+            scratch(3, 4, 4, NZ0, LANES),
             scratch(3, 4, 4, ROWS0, LANES), scratch(3, 4, 4, ROWS0, LANES),
             pltpu.SemaphoreType.DMA((4,)),
         ],
@@ -543,14 +538,14 @@
 def up(c0, v00, v01, g, own, below, above, diag, depth, cells):
     return pl.pallas_call(
         functools.partial(up_kernel, 1.0 / cells),
-        out_shape=[f32(3, 8, 16, LANES), f32(depth, 1, LANES)],
+        out_shape=[f32(3, 8, 16, LANES), f32(depth, 3, 3)],
         in_specs=[HB] * 4 + [VM] * 4,
         out_specs=[VM] * 2,
         scratch_shapes=level_scratch(2, NZ1) + level_scratch(1, NZ2) + level_scratch(1, NZ3, True)
         + [
             scratch(3, 2, 2, 144, LANES), scratch(3, 1, 1, 80, LANES), scratch(3, 1, 1, 80, LANES),
             scratch(3, 4, 4, ROWS0, LANES), scratch(3, 4, 4, ROWS0, LANES),
-            scratch(6, 4, 4, NZ0, LANES), scratch(3, 4, 4, NZ0, LANES), scratch(3, 4, 4, NZ0, LANES),
+            scratch(6, 4, 4, NZ0, LANES), scratch(3, 4, 4, ROWS0, LANES), scratch(3, 4, 4, NZ0, LANES),
             scratch(LANES, LANES), pltpu.SemaphoreType.DMA((4,)),
         ],
         compiler_params=params(),
@@ -582,7 +577,7 @@
     cells = plane * labels.size * depth
     p, sums = up(c0, v00, v01, g, own, below, above, diag, depth, cells)
     parts = lax.all_to_all(sums, "dep", 0, 0)
-    tensor = jnp.sum(parts, axis=(0, 1))[:9].reshape(3, 3)
+    tensor = jnp.sum(parts, axis=0)
     return p, tensor
 
 

time: 102 us -> 103 us (level)
  blocking collectives: 50.1 us -> 51.4 us
    all_to_all x1, blocking collectives: 27.6 us -> 28.8 us  [body(): parts = lax.all_to_all(sums, 'dep', 0, 0)]
    pallas_call x1, Pallas kernels: 13.7 us -> 12.6 us  [up(): pl.pallas_call(functools.partial(up_kernel, 1.0 / cells), out_shape=[f32(...]
    pallas_call x1, Pallas kernels: 10.7 us -> 11.8 us  [down(): pl.pallas_call(down_kernel, out_shape=[f32(6, 4, 4, NZ0, LANES), f32(3, 4...]
where the time goes in v4:
time: 103 us
  blocking collectives  51.4 us (50%)
  Pallas kernels  26.1 us (25%)
  starting transfers between devices  15.6 us (15%)
  waiting for transfers between devices  7.47 us (7%)
  other arithmetic  1.47 us (1%)
    all_to_all x1, blocking collectives, body(): parts = lax.all_to_all(sums, 'dep', 0, 0)  28.8 us
    all_to_all x1, blocking collectives, body(): lax.all_to_all(jnp.broadcast_to(column[None], (plane,) + column.shape), (...  22.5 us
    pallas_call x1, Pallas kernels, up(): pl.pallas_call(functools.partial(up_kernel, 1.0 / cells), out_shape=[f32(...  12.6 us
    pallas_call x1, Pallas kernels, down(): pl.pallas_call(down_kernel, out_shape=[f32(6, 4, 4, NZ0, LANES), f32(3, 4...  11.8 us
    ppermute x2, starting transfers between devices, from_below(): return lax.ppermute(x, 'dep', [(i, i + 1) for i in range(n - 1)])  8.58 us
    ppermute x2, starting transfers between devices, from_above(): return lax.ppermute(x, 'dep', [(i + 1, i) for i in range(n - 1)])  7.06 us
    ppermute x2, waiting for transfers between devices, from_above(): return lax.ppermute(x, 'dep', [(i + 1, i) for i in range(n - 1)])  5.39 us
    ppermute x2, waiting for transfers between devices, from_below(): return lax.ppermute(x, 'dep', [(i, i + 1) for i in range(n - 1)])  2.07 us
  transfers between devices with their start and end apart: 4, of which 3 were waited for; matrix products, arithmetic and copies ran while one was open for 0% of the time, Pallas kernels for 0%

profile of v4, /device:TPU:1, one launch (start us, length us, event | category | flops | bytes accessed | tf_op | source)
XLA Modules:
  0.0 102.8 jit_solution(10331848301858271082)
XLA Ops:
  0.6 1.7 %look_up.1 = (f32[128,128]{1,0:T(8,128)}, f32[4,128]{1,0:T(4,128)}, f32[4,128]{1,0:T(4,128)}) custom-call(s32[8,16,128]{2,1,0:T(8,128)} %labels_ref.1, f32[8]{0:T(128)} %table_ref.1), custom_call_target="tpu_custom_call" | custom-call | tf_op jit(solution)/shard_map/look_up/pallas_call | solution.py:506
  2.3 4.9 %collective-permute-start = (f32[4,128]{1,0:T(4,128)}, f32[4,128]{1,0:T(4,128)S(1)}, u32[]{:S(2)}, u32[]{:S(2)}) collective-permute-start(f32[4,128]{1,0:T(4,128)} %get-tuple-element.15), channel_id=1, source_target_pairs={{0,1},{1,2},{2,3},{3,4},{4,5},{5,6},{6,7},{7,8},{8,9},{9,10},{10,1... | collective-permute-start | bytes 6152 | tf_op jit(solution)/shard_map/ppermute | solution.py:558
  7.2 5.1 %collective-permute-start.1 = (f32[4,128]{1,0:T(4,128)}, f32[4,128]{1,0:T(4,128)S(1)}, u32[]{:S(2)}, u32[]{:S(2)}) collective-permute-start(f32[4,128]{1,0:T(4,128)} %get-tuple-element.17), channel_id=1, source_target_pairs={{1,0},{2,1},{3,2},{4,3},{5,4},{6,5},{7,6},{8,7},{9,8},{10,9},{11,1... | collective-permute-start | bytes 6152 | tf_op jit(solution)/shard_map/ppermute | solution.py:563
  12.4 0.0 collective-permute-done
  12.4 1.0 collective-permute-done.1
  13.4 0.8 pad_maximum_fusion
  14.2 0.1 broadcast_in_dim.2
  14.3 22.5 %all_to_all.10.blocks = f32[16,136,128]{2,1,0:T(8,128)S(1)} all-to-all(f32[16,136,128]{2,1,0:T(8,128)S(1)} %broadcast_in_dim.2), channel_id=1, replica_groups=mesh['row'=4,'col'=4,'dep'=32] {'row','col'}, dimensions={0} | all-to-all | bytes 2228224 | tf_op jit(solution)/shard_map/all_to_all | solution.py:570
  36.8 11.8 %down.1 = (f32[6,4,4,136,128]{4,3,2,1,0:T(8,128)S(1)}, f32[3,4,4,152,128]{4,3,2,1,0:T(8,128)S(1)}, f32[3,4,4,152,128]{4,3,2,1,0:T(8,128)S(1)}, f32[3,4,4,136,128...) custom-call(f32[16,136,128]{2,1,0:T(8,128)S(1)} %all_to_all.10.blocks), custom_call_target="tpu_custom_call" | custom-call | tf_op jit(solution)/shard_map/down/pallas_call | solution.py:517
  48.6 3.7 %collective-permute-start.2 = (f32[4,2,2,40,128]{4,3,2,1,0:T(8,128)S(1)}, f32[4,2,2,40,128]{4,3,2,1,0:T(8,128)S(1)}, u32[]{:S(2)}, u32[]{:S(2)}) collective-permute-start(f32[4,2,2,40,128]{4,3,2,1,0:T(8,128)S(1)} %get-tuple-element.23), channel_id=1, source_target_pairs={{0,1},{1,2},{2,3},{3,4},{4,5},{5,6},{6,7},{7,8},{8,9},{9,10},{10,1... | collective-permute-start | bytes 983048 | tf_op jit(solution)/shard_map/ppermute | solution.py:558
  52.3 1.9 %collective-permute-start.3 = (f32[4,2,2,40,128]{4,3,2,1,0:T(8,128)S(1)}, f32[4,2,2,40,128]{4,3,2,1,0:T(8,128)S(1)}, u32[]{:S(2)}, u32[]{:S(2)}) collective-permute-start(f32[4,2,2,40,128]{4,3,2,1,0:T(8,128)S(1)} %get-tuple-element.24), channel_id=1, source_target_pairs={{1,0},{2,1},{3,2},{4,3},{5,4},{6,5},{7,6},{8,7},{9,8},{10,9},{11,1... | collective-permute-start | bytes 983048 | tf_op jit(solution)/shard_map/ppermute | solution.py:563
  54.2 2.1 %collective-permute-done.2.below = f32[4,2,2,40,128]{4,3,2,1,0:T(8,128)S(1)} collective-permute-done((f32[4,2,2,40,128]{4,3,2,1,0:T(8,128)S(1)}, f32[4,2,2,40,128]{4,3,2,1,0:T(8,128)S(1)}, u32[]{:S(2)}, u32[]{:S(2)}) %collective-permute-start.2) | collective-permute-done | bytes 327712 | tf_op jit(solution)/shard_map/ppermute | solution.py:558
  56.3 4.4 %collective-permute-done.3.above = f32[4,2,2,40,128]{4,3,2,1,0:T(8,128)S(1)} collective-permute-done((f32[4,2,2,40,128]{4,3,2,1,0:T(8,128)S(1)}, f32[4,2,2,40,128]{4,3,2,1,0:T(8,128)S(1)}, u32[]{:S(2)}, u32[]{:S(2)}) %collective-permute-start.3) | collective-permute-done | bytes 327712 | tf_op jit(solution)/shard_map/ppermute | solution.py:563
  60.7 12.6 %up.1 = (f32[3,8,16,128]{3,2,1,0:T(8,128)}, f32[32,3,3]{2,1,0:T(4,128)S(1)}) custom-call(f32[6,4,4,136,128]{4,3,2,1,0:T(8,128)S(1)} %get-tuple-element.18.c_in, f32[3,4,4,152,128]{4,3,2,1,0:T(8,128)S(1)} %get-tuple-element.19.v0_in, f32[3,4,4,152,128]{4,3,2,1,0:T(8,128)S(1)} %get-tuple-element.20.v1_in, f32[3,4,4,136,128]{4,3,2,1,0:T(8,128)S(1)} %get-tuple-element.21.g_in, ...), custom_call_target="tpu_custom_call" | custom-call | tf_op jit(solution)/shard_map/up/pallas_call | solution.py:539
  73.3 28.8 %all_to_all.11 = f32[32,3,3]{2,1,0:T(4,128)S(1)} all-to-all(f32[32,3,3]{2,1,0:T(4,128)S(1)} %get-tuple-element.27), channel_id=1, replica_groups=mesh['row'=4,'col'=4,'dep'=32] {'dep'}, dimensions={0} | all-to-all | bytes 2304 | tf_op jit(solution)/shard_map/all_to_all | solution.py:579
  102.2 0.6 reduce_sum.9
Async XLA Ops:
  2.3 10.1 %collective-permute-start = (f32[4,128]{1,0:T(4,128)}, f32[4,128]{1,0:T(4,128)S(1)}, u32[]{:S(2)}, u32[]{:S(2)}) collective-permute-start(f32[4,128]{1,0:T(4,128)} %get-tuple-element.15), channel_id=1, source_target_pairs={{0,1},{1,2},{2,3},{3,4},{4,5},{5,6},{6,7},{7,8},{8,9},{9,10},{10,1... | collective-permute-start | bytes 6152 | tf_op jit(solution)/shard_map/ppermute | solution.py:558
  7.2 6.2 %collective-permute-start.1 = (f32[4,128]{1,0:T(4,128)}, f32[4,128]{1,0:T(4,128)S(1)}, u32[]{:S(2)}, u32[]{:S(2)}) collective-permute-start(f32[4,128]{1,0:T(4,128)} %get-tuple-element.17), channel_id=1, source_target_pairs={{1,0},{2,1},{3,2},{4,3},{5,4},{6,5},{7,6},{8,7},{9,8},{10,9},{11,1... | collective-permute-start | bytes 6152 | tf_op jit(solution)/shard_map/ppermute | solution.py:563
  48.6 7.7 %collective-permute-start.2 = (f32[4,2,2,40,128]{4,3,2,1,0:T(8,128)S(1)}, f32[4,2,2,40,128]{4,3,2,1,0:T(8,128)S(1)}, u32[]{:S(2)}, u32[]{:S(2)}) collective-permute-start(f32[4,2,2,40,128]{4,3,2,1,0:T(8,128)S(1)} %get-tuple-element.23), channel_id=1, source_target_pairs={{0,1},{1,2},{2,3},{3,4},{4,5},{5,6},{6,7},{7,8},{8,9},{9,10},{10,1... | collective-permute-start | bytes 983048 | tf_op jit(solution)/shard_map/ppermute | solution.py:558
  52.3 8.4 %collective-permute-start.3 = (f32[4,2,2,40,128]{4,3,2,1,0:T(8,128)S(1)}, f32[4,2,2,40,128]{4,3,2,1,0:T(8,128)S(1)}, u32[]{:S(2)}, u32[]{:S(2)}) collective-permute-start(f32[4,2,2,40,128]{4,3,2,1,0:T(8,128)S(1)} %get-tuple-element.24), channel_id=1, source_target_pairs={{1,0},{2,1},{3,2},{4,3},{5,4},{6,5},{7,6},{8,7},{9,8},{10,9},{11,1... | collective-permute-start | bytes 983048 | tf_op jit(solution)/shard_map/ppermute | solution.py:563
